TPU v7x, 128 devices: a whole 4x4x4 slice. The times are simulated.
128 devices in a mesh: gx: 16 (over x, z_hi, core), gy: 8 (over z_lo, y).
Axes of the slice: x: 4, y: 4, z: 4 (z_hi: 2, z_lo: 2; z = z_hi * 2 + z_lo), core: 2. Of those that a mesh axis runs over, the one named last changes fastest.
Arguments:
- features: bfloat16 [112, 168, 2016], P('gx', 'gy'), may hold values from -60 to 60
- labels: int32 [112, 168, 42], P('gx', 'gy'), may hold values 0 or 1
- gain_one: float32 [48], replicated, may hold values from 0.1 to 1.9
- gain_two: float32 [48], replicated, may hold values from 0.1 to 1.9
- w_qkv: bfloat16 [48, 144], replicated, may hold values from -0.875 to 0.875
- w_proj: bfloat16 [48, 48], replicated, may hold values from -0.875 to 0.875
- w_up: bfloat16 [48, 192], replicated, may hold values from -0.875 to 0.875
- w_down: bfloat16 [192, 48], replicated, may hold values from -0.4375 to 0.4375
- w_head: bfloat16 [48, 2], replicated, may hold values from -0.875 to 0.875
Outputs:
- grad_features: bfloat16 [112, 168, 2016], P('gx', 'gy')
- grad_qkv: float32 [48, 144], replicated
- grad_proj: float32 [48, 48], replicated
- grad_up: float32 [48, 192], replicated
- grad_down: float32 [192, 48], replicated
- grad_head: float32 [48, 2], replicated
All inputs are finite; a program needn't handle non-finite values. No bound on the sum of `labels` on one device may be relied on, other than what follows from the above.
Results may differ from a plain program's by a relative error of at most 0.0056.
The roundings to bfloat16 on the way count: a program that leaves them out, or rounds other values in their place, can miss the bound.
Values may be sent and summed in bfloat16 or wider, within the bound.
A program may use at most 64 MiB of HBM per device.

v0:
```python
import math

import jax
import jax.numpy as jnp
from jax import lax
from jax.sharding import PartitionSpec as P

HEADS = 3
WIN = 7
SHIFT = 3


EPS = 1e-05
HI = lax.Precision.HIGHEST


def passed_along(x, axis, by):
    devices = lax.axis_size(axis)
    return lax.ppermute(x, axis, [(i, (i + by) % devices) for i in range(devices)])


def rounded(values):
    return lax.optimization_barrier(values.astype(jnp.bfloat16)).astype(jnp.float32)


def layer_norm(values, gain):
    centre = jnp.mean(values, axis=-1, keepdims=True)
    spread = values - centre
    second = jnp.mean(spread * spread, axis=-1, keepdims=True)
    return spread * lax.rsqrt(second + EPS) * gain


def attend(normed, region, w_qkv, w_proj):
    blocks, points, width = normed.shape
    head_dim = width // HEADS
    packed = rounded(jnp.einsum("bpc,cf->bpf", normed.astype(jnp.float32), w_qkv, precision=HI))
    packed = packed.reshape(blocks, points, 3, HEADS, head_dim).astype(jnp.bfloat16)
    query = packed[:, :, 0]
    keys = packed[:, :, 1]
    value = packed[:, :, 2]
    scores = jnp.einsum(
        "bphd,bqhd->bhpq", query, keys, preferred_element_type=jnp.float32
    ) * head_dim ** (-0.5)
    allowed = (region[:, :, None] == region[:, None, :])[:, None]
    raw = jnp.where(allowed, jnp.exp(scores), 0.0)
    weights = lax.optimization_barrier(
        (raw / jnp.sum(raw, axis=-1, keepdims=True)).astype(jnp.bfloat16)
    )
    mixed = rounded(
        jnp.einsum("bhpq,bqhd->bphd", weights, value, preferred_element_type=jnp.float32)
    )
    mixed = mixed.reshape(blocks, points, width)
    return jnp.einsum("bpc,cf->bpf", mixed, w_proj, precision=HI).astype(jnp.bfloat16)


def finish(resid, attn_out, marks, gain_two, w_up, w_down, w_head):
    state = rounded(resid + attn_out.astype(jnp.float32))
    normed = rounded(layer_norm(state, gain_two))
    inner = rounded(jax.nn.gelu(jnp.einsum("...c,cf->...f", normed, w_up, precision=HI)))
    result = rounded(state + jnp.einsum("...c,cf->...f", inner, w_down, precision=HI))
    logits = jnp.einsum("...c,cf->...f", result, w_head, precision=HI)
    sign = 1.0 - 2.0 * marks.astype(jnp.float32)
    return jnp.sum(jax.nn.softplus((logits[..., 1] - logits[..., 0]) * sign))


def to_windows(values):
    size_x, size_y, size_z = values.shape[:3]
    rest = values.shape[3:]
    cut = values.reshape((size_x // WIN, WIN, size_y // WIN, WIN, size_z // WIN, WIN) + rest)
    order = (0, 2, 4, 1, 3, 5) + tuple(range(6, 6 + len(rest)))
    return cut.transpose(order).reshape((-1, WIN**3) + rest)


def from_windows(values, size_x, size_y, size_z):
    rest = values.shape[2:]
    cut = values.reshape((size_x // WIN, size_y // WIN, size_z // WIN, WIN, WIN, WIN) + rest)
    order = (0, 3, 1, 4, 2, 5) + tuple(range(6, 6 + len(rest)))
    return cut.transpose(order).reshape((size_x, size_y, size_z) + rest)


def region_ids(count, offset, total):
    place = offset + jnp.arange(count, dtype=jnp.int32)
    return (place >= total - WIN).astype(jnp.int32) + (place >= total - SHIFT).astype(jnp.int32)


def roll_tiles(values, step):
    edge = values[:SHIFT] if step < 0 else values[-SHIFT:]
    came = passed_along(edge, "gx", step)
    if step < 0:
        values = jnp.concatenate([values[SHIFT:], came], 0)
    else:
        values = jnp.concatenate([came, values[:-SHIFT]], 0)
    edge = values[:, :SHIFT] if step < 0 else values[:, -SHIFT:]
    came = passed_along(edge, "gy", step)
    if step < 0:
        values = jnp.concatenate([values[:, SHIFT:], came], 1)
    else:
        values = jnp.concatenate([came, values[:, :-SHIFT]], 1)
    return jnp.roll(values, step * SHIFT, axis=2)


def body(features, labels, gain_one, gain_two, w_qkv, w_proj, w_up, w_down, w_head):
    tile_x, tile_y, packed = features.shape
    width = gain_one.shape[0]
    depth = packed // width
    total_x = tile_x * lax.axis_size("gx")
    total_y = tile_y * lax.axis_size("gy")
    tokens = total_x * total_y * depth
    grid = features.reshape(tile_x, tile_y, depth, width)
    weights = tuple((w.astype(jnp.float32) for w in (w_qkv, w_proj, w_up, w_down, w_head)))
    region = (
        region_ids(tile_x, lax.axis_index("gx") * tile_x, total_x)[:, None, None] * 9
        + region_ids(tile_y, lax.axis_index("gy") * tile_y, total_y)[None, :, None] * 3
        + region_ids(depth, 0, depth)[None, None, :]
    )
    per = depth // WIN

    def split(values):
        return values.reshape((-1, per) + values.shape[1:])

    regions = split(to_windows(region))
    resid = grid.astype(jnp.float32)
    normed, pull_norm = jax.vjp(
        lambda values: layer_norm(values, gain_one).astype(jnp.bfloat16), resid
    )
    normed_win = split(to_windows(roll_tiles(normed, -1)))

    def forward_fn(piece):
        return attend(piece[0], piece[1], weights[0], weights[1])

    attn_win = lax.map(forward_fn, (normed_win, regions))
    attn_out = roll_tiles(
        from_windows(attn_win.reshape(-1, WIN**3, width), tile_x, tile_y, depth), 1
    )

    def rest(values, attn, up, down, head):
        return finish(values, attn, labels, gain_two, up, down, head)

    _, pull_rest = jax.vjp(rest, resid, attn_out, weights[2], weights[3], weights[4])
    cot_resid, cot_attn, grad_up, grad_down, grad_head = pull_rest(jnp.ones((), jnp.float32))
    cot_attn_win = split(to_windows(roll_tiles(cot_attn, -1)))

    def backward_fn(carry, piece):
        part_n, part_r, part_c = piece

        def local(values, qkv, proj):
            return attend(values, part_r, qkv, proj)

        _, pull = jax.vjp(local, part_n, weights[0], weights[1])
        cot_n, grad_qkv, grad_proj = pull(part_c)
        return ((carry[0] + grad_qkv, carry[1] + grad_proj), cot_n)

    start = (jnp.zeros(weights[0].shape, jnp.float32), jnp.zeros(weights[1].shape, jnp.float32))
    (grad_qkv, grad_proj), cot_norm_win = lax.scan(
        backward_fn, start, (normed_win, regions, cot_attn_win)
    )
    cot_normed = roll_tiles(
        from_windows(cot_norm_win.reshape(-1, WIN**3, width), tile_x, tile_y, depth), 1
    )
    (cot_layer,) = pull_norm(cot_normed)
    back = (cot_resid + cot_layer).astype(jnp.bfloat16)
    sums = (grad_qkv, grad_proj, grad_up, grad_down, grad_head)
    totals = lax.psum((sums[0], sums[1], sums[2], sums[3], sums[4]), ("gx", "gy"))
    scale = 1.0 / math.sqrt(tokens)
    return (
        back.reshape(tile_x, tile_y, packed),
        totals[0] * scale,
        totals[1] * scale,
        totals[2] * scale,
        totals[3] * scale,
        totals[4] * scale,
    )


def solution(mesh):
    placed = (P("gx", "gy", None), P("gx", "gy", None), P(), P(), P(), P(), P(), P(), P())
    return jax.shard_map(
        body,
        mesh=mesh,
        in_specs=placed,
        out_specs=(P("gx", "gy", None), P(), P(), P(), P(), P()),
        check_vma=False,
    )
```

profile of v0, /device:TPU:1, one launch (start us, length us, event | category | flops | bytes accessed | tf_op | source)
XLA Modules:
  0.0 446.9 jit_solution(10627157293510208919)
XLA Ops:
  7.2 4.2 reshape.193
  14.5 3.9 multiply_reduce_fusion.1
  25.2 11.3 %collective-permute-done = bf16[3,21,42,48]{3,2,1,0:T(8,128)(2,1)S(1)} collective-permute-done((bf16[3,21,42,48]{3,2,1,0:T(8,128)(2,1)S(1)}, bf16[3,21,42,48]{3,2,1,0:T(8,128)(2,1)S(1)}, u32[]{:S(2)}, u32[]{:S(2)}) %collective-permute-start) | collective-permute-done | bytes 254048 | tf_op jit(solution)/shard_map/ppermute | solution.py:19
  36.6 3.5 collective-permute-start.1
  53.9 37.5 %while.25 = (s32[]{:T(128)}, bf16[3,6,343,48]{2,3,1,0:T(8,128)(2,1)S(1)}, bf16[3,6,343,48]{2,3,1,0:T(8,128)(2,1)S(1)}, f32[48,144]{1,0:T(8,128)S(1)}, s32[3,6,34...) while((s32[]{:T(128)}, bf16[3,6,343,48]{2,3,1,0:T(8,128)(2,1)S(1)}, ...), condition=%wide.region_4.5_spmd, body=%wide.region_2.4_spmd.sunk | while | flops 379147392 | bytes 30401928 | solution.py:131
  55.3 5.1 %fusion.151 = (f32[6,3,343]{2,1,0:T(4,128)S(1)}, f32[6,3,343,343]{2,3,1,0:T(8,128)}) fusion(pred[6,343,343]{1,2,0:T(8,128)(4,1)S(1)} %broadcast_compare_fusion.4, bf16[6,343,3,3,16]{1,4,3,2,0:T(8,128)(2,1)S(1)} %bitcast.297), kind=kOutput, calls=%fused_computation.2.clone.1 | convolution fusion | flops 74112688 | bytes 9730368 | tf_op jit(solution)/shard_map/while/body/eval_jaxpr/bphd,bqhd->bhpq/dot_general | solution.py:41
  60.4 4.8 %divide_convert_fusion.4 = bf16[6,3,343,343]{2,3,1,0:T(8,128)(2,1)S(1)} fusion(f32[6,3,343,343]{2,3,1,0:T(8,128)} %get-tuple-element.276, f32[6,3,343]{2,1,0:T(4,128)S(1)} %get-tuple-element.277, pred[6,343,343]{1,2,0:T(8,128)(4,1)S(1)} %broadcast_compare_fusion.4), kind=kLoop, calls=%fused_computation.clone.1 | loop fusion | flops 8470728 | bytes 13436682 | tf_op jit(solution)/shard_map/while/body/eval_jaxpr/convert_element_type | solution.py:47
  67.8 5.1 %fusion.151 = (f32[6,3,343]{2,1,0:T(4,128)S(1)}, f32[6,3,343,343]{2,3,1,0:T(8,128)}) fusion(pred[6,343,343]{1,2,0:T(8,128)(4,1)S(1)} %broadcast_compare_fusion.4, bf16[6,343,3,3,16]{1,4,3,2,0:T(8,128)(2,1)S(1)} %bitcast.297), kind=kOutput, calls=%fused_computation.2.clone.1 | convolution fusion | flops 74112688 | bytes 9730368 | tf_op jit(solution)/shard_map/while/body/eval_jaxpr/bphd,bqhd->bhpq/dot_general | solution.py:41
  72.9 4.8 %divide_convert_fusion.4 = bf16[6,3,343,343]{2,3,1,0:T(8,128)(2,1)S(1)} fusion(f32[6,3,343,343]{2,3,1,0:T(8,128)} %get-tuple-element.276, f32[6,3,343]{2,1,0:T(4,128)S(1)} %get-tuple-element.277, pred[6,343,343]{1,2,0:T(8,128)(4,1)S(1)} %broadcast_compare_fusion.4), kind=kLoop, calls=%fused_computation.clone.1 | loop fusion | flops 8470728 | bytes 13436682 | tf_op jit(solution)/shard_map/while/body/eval_jaxpr/convert_element_type | solution.py:47
  80.3 5.1 %fusion.151 = (f32[6,3,343]{2,1,0:T(4,128)S(1)}, f32[6,3,343,343]{2,3,1,0:T(8,128)}) fusion(pred[6,343,343]{1,2,0:T(8,128)(4,1)S(1)} %broadcast_compare_fusion.4, bf16[6,343,3,3,16]{1,4,3,2,0:T(8,128)(2,1)S(1)} %bitcast.297), kind=kOutput, calls=%fused_computation.2.clone.1 | convolution fusion | flops 74112688 | bytes 9730368 | tf_op jit(solution)/shard_map/while/body/eval_jaxpr/bphd,bqhd->bhpq/dot_general | solution.py:41
  85.4 4.8 %divide_convert_fusion.4 = bf16[6,3,343,343]{2,3,1,0:T(8,128)(2,1)S(1)} fusion(f32[6,3,343,343]{2,3,1,0:T(8,128)} %get-tuple-element.276, f32[6,3,343]{2,1,0:T(4,128)S(1)} %get-tuple-element.277, pred[6,343,343]{1,2,0:T(8,128)(4,1)S(1)} %broadcast_compare_fusion.4), kind=kLoop, calls=%fused_computation.clone.1 | loop fusion | flops 8470728 | bytes 13436682 | tf_op jit(solution)/shard_map/while/body/eval_jaxpr/convert_element_type | solution.py:47
  98.4 8.6 %collective-permute-done.2 = bf16[3,21,42,48]{3,2,1,0:T(8,128)(2,1)S(1)} collective-permute-done((bf16[3,21,42,48]{3,2,1,0:T(8,128)(2,1)}, bf16[3,21,42,48]{3,2,1,0:T(8,128)(2,1)S(1)}, u32[]{:S(2)}, u32[]{:S(2)}) %collective-permute-start.2) | collective-permute-done | bytes 254048 | tf_op jit(solution)/shard_map/ppermute | solution.py:19
  108.0 7.3 %collective-permute-done.3 = bf16[7,3,42,48]{3,2,1,0:T(8,128)(2,1)S(1)} collective-permute-done((bf16[7,3,42,48]{3,2,1,0:T(8,128)(2,1)S(1)}, bf16[7,3,42,48]{3,2,1,0:T(8,128)(2,1)S(1)}, u32[]{:S(2)}, u32[]{:S(2)}) %collective-permute-start.3) | collective-permute-done | bytes 84704 | tf_op jit(solution)/shard_map/ppermute | solution.py:19
  134.4 5.2 %fusion.44 = f32[7,21,42,192]{3,2,1,0:T(8,128)S(1)} fusion(bf16[7,21,42,192]{3,2,1,0:T(8,128)(2,1)S(1)} %convolution_convert_fusion.11, f32[7,21,42,192]{3,2,1,0:T(8,128)S(1)} %get-tuple-element.186), kind=kLoop, calls=%fused_computation.79 | loop fusion | flops 23708160 | bytes 11854080 | tf_op jit(solution)/shard_map/transpose(jvp())/add_any | solution.py:59
  139.6 3.8 convolution_bitcast_fusion.3
  143.4 3.4 convolution_convert_fusion.13
  149.1 4.4 fusion.61
  153.5 4.6 %add_convert_fusion.1 = bf16[7,21,42,48]{3,2,1,0:T(8,128)(2,1)S(1)} fusion(bf16[7,21,42,48]{3,2,1,0:T(8,128)(2,1)S(1)} %convolution_convert_fusion.12, bf16[7,21,42,48]{3,2,1,0:T(8,128)(2,1)S(1)} %add_convert_fusion.2, bf16[7,21,42,48]{3,2,1,0:T(8,128)(2,1)S(1)} %convolution_convert_fusion.13, f32[7,21,42]{2,1,0:T(8,128)S(1)} %negate_multiply_fusion.1, ...), kind=kLoop, calls=%fused_computation.105 | loop fusion | flops 3556224 | bytes 2469792 | tf_op jit(solution)/shard_map/transpose(jvp())/convert_element_type | solution.py:23
  158.1 9.4 %collective-permute-start.4 = (bf16[3,21,42,48]{3,2,1,0:T(8,128)(2,1)S(1)}, bf16[3,21,42,48]{3,2,1,0:T(8,128)(2,1)S(1)}, u32[]{:S(2)}, u32[]{:S(2)}) collective-permute-start(bf16[3,21,42,48]{3,2,1,0:T(8,128)(2,1)S(1)} %slice.164), channel_id=1, source_target_pairs={{0,120},{8,0},{16,8},{24,16},{32,24},{40,32},{48,40},{56,48},{64,5... | collective-permute-start | bytes 762056 | tf_op jit(solution)/shard_map/ppermute | solution.py:19
  175.6 3.4 collective-permute-done.5
  181.4 3.9 reshape.191
  188.3 3.8 reshape_reshape.18
  194.9 59.9 %while.26 = (s32[]{:T(128)}, f32[48,144]{1,0:T(8,128)S(1)}, f32[48,48]{1,0:T(8,128)S(1)}, bf16[3,6,343,48]{2,3,1,0:T(8,128)(2,1)}, bf16[3,6,343,48]{2,3,1,0:T(8,...) while((s32[]{:T(128)}, f32[48,144]{1,0:T(8,128)S(1)}, ...), condition=%wide.region_12.13_spmd.clone, body=%wide.region_9.12_spmd.clone.sunk | while | flops 887193472 | bytes 76765360 | solution.py:154
  201.6 3.5 divide_convert_fusion.5
  221.5 3.5 divide_convert_fusion.5
  241.4 3.5 divide_convert_fusion.5
  257.9 4.0 reshape_reshape.19
  269.0 137.2 %all-reduce.8.cloned.1.call-done = (f32[48,144]{1,0:T(8,128)}, f32[48,48]{1,0:T(8,128)}, f32[48,192]{1,0:T(8,128)}, f32[192,48]{0,1:T(8,128)}, f32[48,2]{0,1:T(2,128)}) async-done(((f32[48,144]{1,0:T(8,128)}, f32[48,48]{1,0:T(8,128)}, f32[48,192]{1,0:T(8,128)}, f32[192,48]{0,1:T(8,128)}, f32[48,2]{0,1:T(2,128)}), (f32[48,144]{1,0:T(8,128)}, f32[48,48]{1,0:T(8,128)}, f32[48,192]{1,0:T(8,128)}, ...) | async-done | bytes 110992 | tf_op jit(solution)/shard_map/psum | solution.py:163
  414.4 8.6 %collective-permute-done.7 = bf16[7,3,42,48]{3,2,1,0:T(8,128)(2,1)S(1)} collective-permute-done((bf16[7,3,42,48]{3,2,1,0:T(8,128)(2,1)S(1)}, bf16[7,3,42,48]{3,2,1,0:T(8,128)(2,1)S(1)}, u32[]{:S(2)}, u32[]{:S(2)}) %collective-permute-start.7) | collective-permute-done | bytes 84704 | tf_op jit(solution)/shard_map/ppermute | solution.py:19
  425.9 4.5 fusion.70
  430.4 5.3 %add_convert_fusion = bf16[7,21,42,48]{3,2,1,0:T(8,128)(2,1)} fusion(bf16[7,21,42,48]{3,2,1,0:T(8,128)(2,1)S(1)} %add_convert_fusion.1, f32[7,21,42]{2,1,0:T(8,128)S(1)} %negate_multiply_fusion, f32[7,21,42]{2,1,0:T(8,128)S(1)} %multiply_multiply_fusion.2, f32[7,21,42,48]{3,2,1,0:T(8,128)S(1)} %copy-done.3, f32[7,21,42]{2,1,0:T(8,128)S(1)} %copy-done.6, ...), kind=kLoop, calls=%fused_computation.102 | loop fusion | flops 5334336 | bytes 3062496 | tf_op jit(solution)/shard_map/convert_element_type | solution.py:161
  435.7 4.0 reshape.192
  (207 shorter events, 146.7 us)
Async XLA Ops:
  7.2 116.9 %copy-start = (bf16[48,192]{1,0:T(8,128)(2,1)S(1)}, bf16[48,192]{1,0:T(8,128)(2,1)}, u32[]{:S(2)}) copy-start(bf16[48,192]{1,0:T(8,128)(2,1)} %param.19) | copy-start | bytes 55300
  7.2 399.0 %all-reduce.8.cloned.1.call-start = ((), (), s32[]{:S(2)}) async-start(), calls=%async_computation | async-start | bytes 346112 | tf_op jit(solution)/shard_map/psum | solution.py:163
  11.4 7.0 %copy-start.18 = (f32[48]{0:T(128)S(1)}, f32[48]{0:T(128)}, u32[]{:S(2)}) copy-start(f32[48]{0:T(128)} %param.15) | copy-start | bytes 580
  14.5 4.0 copy-start.2
  14.5 6.1 %copy-start.5 = (f32[7,21,42]{2,1,0:T(8,128)}, f32[7,21,42]{2,1,0:T(8,128)S(1)}, u32[]{:S(2)}) copy-start(f32[7,21,42]{2,1,0:T(8,128)S(1)} %broadcast_multiply_fusion.1) | copy-start | bytes 74092
  18.4 3.5 copy-start.11
  18.4 6.4 %copy-start.8 = (f32[7,21,42]{2,1,0:T(8,128)}, f32[7,21,42]{2,1,0:T(8,128)S(1)}, u32[]{:S(2)}) copy-start(f32[7,21,42]{2,1,0:T(8,128)S(1)} %fusion.76) | copy-start | bytes 74092
  18.4 6.4 %copy-start.15 = (bf16[48,48]{1,0:T(8,128)(2,1)S(1)}, bf16[48,48]{1,0:T(8,128)(2,1)}, u32[]{:S(2)}) copy-start(bf16[48,48]{1,0:T(8,128)(2,1)} %param.18) | copy-start | bytes 13828
  18.4 6.4 %copy-start.16 = (bf16[48,144]{1,0:T(8,128)(2,1)S(1)}, bf16[48,144]{1,0:T(8,128)(2,1)}, u32[]{:S(2)}) copy-start(bf16[48,144]{1,0:T(8,128)(2,1)} %param.17) | copy-start | bytes 41476
  20.6 1.2 copy-start.4
  21.9 14.6 %collective-permute-start = (bf16[3,21,42,48]{3,2,1,0:T(8,128)(2,1)S(1)}, bf16[3,21,42,48]{3,2,1,0:T(8,128)(2,1)S(1)}, u32[]{:S(2)}, u32[]{:S(2)}) collective-permute-start(bf16[3,21,42,48]{3,2,1,0:T(8,128)(2,1)S(1)} %slice.152), channel_id=1, source_target_pairs={{0,120},{8,0},{16,8},{24,16},{32,24},{40,32},{48,40},{56,48},{64,5... | collective-permute-start | bytes 762056 | tf_op jit(solution)/shard_map/ppermute | solution.py:19
  36.6 7.1 %collective-permute-start.1 = (bf16[7,3,42,48]{3,2,1,0:T(8,128)(2,1)S(1)}, bf16[7,3,42,48]{3,2,1,0:T(8,128)(2,1)S(1)}, u32[]{:S(2)}, u32[]{:S(2)}) collective-permute-start(bf16[7,3,42,48]{3,2,1,0:T(8,128)(2,1)S(1)} %pad_maximum_fusion.7), channel_id=1, source_target_pairs={{0,7},{1,0},{2,1},{3,2},{4,3},{5,4},{6,5},{7,6},{8,15},{9,8},{10,9... | collective-permute-start | bytes 254024 | tf_op jit(solution)/shard_map/ppermute | solution.py:19
  97.0 10.0 %collective-permute-start.2 = (bf16[3,21,42,48]{3,2,1,0:T(8,128)(2,1)}, bf16[3,21,42,48]{3,2,1,0:T(8,128)(2,1)S(1)}, u32[]{:S(2)}, u32[]{:S(2)}) collective-permute-start(bf16[3,21,42,48]{3,2,1,0:T(8,128)(2,1)} %slice.119), channel_id=1, source_target_pairs={{0,8},{8,16},{16,24},{24,32},{32,40},{40,48},{48,56},{56,64},{64,7... | collective-permute-start | bytes 762056 | tf_op jit(solution)/shard_map/ppermute | solution.py:19
  107.4 7.9 %collective-permute-start.3 = (bf16[7,3,42,48]{3,2,1,0:T(8,128)(2,1)S(1)}, bf16[7,3,42,48]{3,2,1,0:T(8,128)(2,1)S(1)}, u32[]{:S(2)}, u32[]{:S(2)}) collective-permute-start(bf16[7,3,42,48]{3,2,1,0:T(8,128)(2,1)S(1)} %slice.159), channel_id=1, source_target_pairs={{0,1},{1,2},{2,3},{3,4},{4,5},{5,6},{6,7},{7,0},{8,9},{9,10},{10,1... | collective-permute-start | bytes 254024 | tf_op jit(solution)/shard_map/ppermute | solution.py:19
  118.4 3.3 copy-start.17
  124.0 3.1 copy-start.13
  127.2 1.1 copy-start.20
  127.2 3.0 copy-start.14
  158.1 15.6 %collective-permute-start.4 = (bf16[3,21,42,48]{3,2,1,0:T(8,128)(2,1)S(1)}, bf16[3,21,42,48]{3,2,1,0:T(8,128)(2,1)S(1)}, u32[]{:S(2)}, u32[]{:S(2)}) collective-permute-start(bf16[3,21,42,48]{3,2,1,0:T(8,128)(2,1)S(1)} %slice.164), channel_id=1, source_target_pairs={{0,120},{8,0},{16,8},{24,16},{32,24},{40,32},{48,40},{56,48},{64,5... | collective-permute-start | bytes 762056 | tf_op jit(solution)/shard_map/ppermute | solution.py:19
  173.8 5.2 %collective-permute-start.5 = (bf16[7,3,42,48]{3,2,1,0:T(8,128)(2,1)S(1)}, bf16[7,3,42,48]{3,2,1,0:T(8,128)(2,1)S(1)}, u32[]{:S(2)}, u32[]{:S(2)}) collective-permute-start(bf16[7,3,42,48]{3,2,1,0:T(8,128)(2,1)S(1)} %pad_maximum_fusion.6), channel_id=1, source_target_pairs={{0,7},{1,0},{2,1},{3,2},{4,3},{5,4},{6,5},{7,6},{8,15},{9,8},{10,9... | collective-permute-start | bytes 254024 | tf_op jit(solution)/shard_map/ppermute | solution.py:19
  254.8 0.6 copy-start.7
  254.8 0.6 copy-start.10
  268.0 143.9 %collective-permute-start.6 = (bf16[3,21,42,48]{3,2,1,0:T(8,128)(2,1)}, bf16[3,21,42,48]{3,2,1,0:T(8,128)(2,1)}, u32[]{:S(2)}, u32[]{:S(2)}) collective-permute-start(bf16[3,21,42,48]{3,2,1,0:T(8,128)(2,1)} %slice.135), channel_id=1, source_target_pairs={{0,8},{8,16},{16,24},{24,32},{32,40},{40,48},{48,56},{56,64},{64,7... | collective-permute-start | bytes 762056 | tf_op jit(solution)/shard_map/ppermute | solution.py:19
  406.2 7.5 %copy-start.21 = (f32[48,2]{0,1:T(2,128)S(1)}, f32[48,2]{0,1:T(2,128)}, u32[]{:S(2)}) copy-start(f32[48,2]{0,1:T(2,128)} %get-tuple-element.176) | copy-start | bytes 1156
  410.4 12.6 %copy-start.3 = (f32[7,21,42,48]{3,2,1,0:T(8,128)S(1)}, f32[7,21,42,48]{3,2,1,0:T(8,128)}, u32[]{:S(2)}) copy-start(f32[7,21,42,48]{3,2,1,0:T(8,128)} %reshape.193) | copy-start | bytes 3556228
  410.4 12.6 %copy-start.6 = (f32[7,21,42]{2,1,0:T(8,128)S(1)}, f32[7,21,42]{2,1,0:T(8,128)}, u32[]{:S(2)}) copy-start(f32[7,21,42]{2,1,0:T(8,128)} %copy-done.5) | copy-start | bytes 74092
  410.4 12.6 %copy-start.19 = (f32[48]{0:T(128)S(1)}, f32[48]{0:T(128)}, u32[]{:S(2)}) copy-start(f32[48]{0:T(128)} %param.15) | copy-start | bytes 580
  413.4 9.6 %collective-permute-start.7 = (bf16[7,3,42,48]{3,2,1,0:T(8,128)(2,1)S(1)}, bf16[7,3,42,48]{3,2,1,0:T(8,128)(2,1)S(1)}, u32[]{:S(2)}, u32[]{:S(2)}) collective-permute-start(bf16[7,3,42,48]{3,2,1,0:T(8,128)(2,1)S(1)} %slice.171), channel_id=1, source_target_pairs={{0,1},{1,2},{2,3},{3,4},{4,5},{5,6},{6,7},{7,0},{8,9},{9,10},{10,1... | collective-permute-start | bytes 254024 | tf_op jit(solution)/shard_map/ppermute | solution.py:19
  414.3 11.6 %copy-start.12 = (f32[7,21,42]{2,1,0:T(8,128)S(1)}, f32[7,21,42]{2,1,0:T(8,128)}, u32[]{:S(2)}) copy-start(f32[7,21,42]{2,1,0:T(8,128)} %copy-done.11) | copy-start | bytes 74092
  414.4 11.5 %copy-start.9 = (f32[7,21,42]{2,1,0:T(8,128)S(1)}, f32[7,21,42]{2,1,0:T(8,128)}, u32[]{:S(2)}) copy-start(f32[7,21,42]{2,1,0:T(8,128)} %copy-done.8) | copy-start | bytes 74092
  430.4 9.3 %copy-start.1 = (bf16[48,192]{1,0:T(8,128)(2,1)S(1)}, bf16[48,192]{1,0:T(8,128)(2,1)}, u32[]{:S(2)}) copy-start(bf16[48,192]{1,0:T(8,128)(2,1)} %param.19) | copy-start | bytes 55300
Sparse Core Ops, SparseCore 0:
  255.5 150.5 all-reduce.7
where the time goes:
time: 452 us; the launch traced here: 447 us
  waiting for transfers between devices  183 us (40%)
  other arithmetic  98.5 us (22%)
  matrix products  77.3 us (17%)
  local copies, waits for them, and re-layouts  53.9 us (12%)
  starting transfers between devices  18.6 us (4%)
  between operations  15.2 us (3%)
    psum x1, waiting for transfers between devices, body(): lax.psum((sums[0], sums[1], sums[2], sums[3], sums[4]), ('gx', 'gy'))  137 us
    ppermute x8, waiting for transfers between devices, passed_along(): lax.ppermute(x, axis, [(i, (i + by) % devices) for i in range(devices)])  45.7 us
    dot_general x12, matrix products, attend(): jnp.einsum('bphd,bqhd->bhpq', query, keys, preferred_element_type=jnp.flo...  31.1 us
    convert_element_type x6, other arithmetic, attend(): (raw / jnp.sum(raw, axis=-1, keepdims=True)).astype(jnp.bfloat16)  25 us
    ppermute x8, starting transfers between devices, passed_along(): lax.ppermute(x, axis, [(i, (i + by) % devices) for i in range(devices)])  18.5 us
    dot_general x12, matrix products, attend(): jnp.einsum('bhpq,bqhd->bphd', weights, value, preferred_element_type=jnp....  14.7 us
    reshape x4, local copies, waits for them, and re-layouts, to_windows(): values.reshape((size_x // WIN, WIN, size_y // WIN, WIN, size_z // WIN, WI...  11.2 us
    dot_general x3, matrix products, finish(): jnp.einsum('...c,cf->...f', normed, w_up, precision=HI)  10.3 us
  transfers between devices with their start and end apart: 9, of which 8 were waited for; matrix products, arithmetic and copies ran while one was open for 6% of the time, Pallas kernels for 0%

commit v1 on v0

v1 whole, which is shorter than its diff:
```python
import math

import jax
import jax.numpy as jnp
from jax import lax
from jax.experimental import pallas as pl
from jax.experimental.pallas import tpu as pltpu
from jax.sharding import PartitionSpec as P

BF = jnp.bfloat16
F32 = jnp.float32
C = 48
FF = 192
NH = 3
WIN = 7
SHIFT = 3
DEPTH = 42
WIDTH = DEPTH * C
LAB = 2048
LW = 2176
KP = 352
TL = 384
PT = 343
NZ = 6
NWY = 3
EPS = 1e-5
BIG = 2.0**100
LOG2E_4 = 0.25 * math.log2(math.e)
CH = [(0, 256), (256, 512), (512, 768), (768, 1024), (1024, 1152)]
GC1 = math.sqrt(2 / math.pi)
GC2 = 0.044715 * GC1
MESH = pl.DeviceIdType.MESH


def dot(a,b): return lax.dot_general(a,b,(((1,),(0,)),((),())),preferred_element_type=F32)
def dot_t(a,b): return lax.dot_general(a,b,(((1,),(1,)),((),())),preferred_element_type=F32)
def split3(v):
    a=v.astype(BF); r=v-a.astype(F32); b=r.astype(BF); r=r-b.astype(F32); return a,b,r.astype(BF)
def mean0(v): return jnp.sum(v,axis=0,keepdims=True)*(1.0/C)
def norm(v):
    s=v-mean0(v)
    r=lax.rsqrt(mean0(s*s)+EPS)
    return s*r, r
def norm_back(d,xh,r):
    return (d-mean0(d)-xh*mean0(d*xh))*r

def scratch():
    return dict(
      qkvT=pltpu.VMEM((144,C),BF), projT=pltpu.VMEM((C,C),BF), upT=pltpu.VMEM((FF,C),BF), downT=pltpu.VMEM((C,FF),BF),
      wx=pltpu.VMEM((64,512),BF), kmask=pltpu.VMEM((16,TL),BF), qmask=pltpu.VMEM((16,TL),F32),
      g1=pltpu.VMEM((C,1),F32), g2=pltpu.VMEM((C,1),F32), wd=pltpu.VMEM((C,1),F32),
      a_up=pltpu.VMEM((C,FF),F32), a_down=pltpu.VMEM((C,FF),F32), a_qkv=pltpu.VMEM((C,144),F32), a_proj=pltpu.VMEM((C,C),F32), a_head=pltpu.VMEM((C,128),F32),
    )
def win_scratch():
    return dict(qblk=pltpu.VMEM((160,1152),BF), oblk=pltpu.VMEM((64,1152),BF), P=pltpu.VMEM((KP,1152),BF), D=pltpu.VMEM((KP,1152),BF),
       qt=pltpu.VMEM((1152,C),BF), ot=pltpu.VMEM((1152,C),BF), dkv=pltpu.VMEM((TL,256),BF))

def init(S, Ws, wqkv, wproj, wup, wdown, whead, g1, g2):
    S['qkvT'][...]=wqkv[...].T
    S['projT'][...]=wproj[...].T
    S['upT'][...]=wup[...].T
    S['downT'][...]=wdown[...].T
    wq=wqkv[...].astype(F32)
    wk=wq[:,48:96]; wv=wq[:,96:144]
    z=lambda n: jnp.zeros((C,n),F32)
    top=jnp.concatenate([wk,wk,wk,z(112),wv,z(80),wq[:,0:48],z(80)],axis=1)
    r=lax.broadcasted_iota(jnp.int32,(16,512),0); l=lax.broadcasted_iota(jnp.int32,(16,512),1)
    bot=((l==144+r)|((l>=304)&(l<307)&(r==7))).astype(F32)
    S['wx'][...]=jnp.concatenate([top,bot],axis=0).astype(BF)
    t=lax.broadcasted_iota(jnp.int32,(16,TL),1); r=lax.broadcasted_iota(jnp.int32,(16,TL),0)
    bz=(t>=4*49).astype(F32)
    u=t-49*sum((t>=49*k).astype(jnp.int32) for k in range(1,7))
    bx=(u>=28).astype(F32)
    v=u-7*sum((u>=7*k).astype(jnp.int32) for k in range(1,7))
    by=(v>=4).astype(F32)
    b=jnp.where(r<2,bx,jnp.where(r<4,by,bz))
    first=(r%2)==0
    S['kmask'][...]=jnp.where(r<6,jnp.where(first,1.0-b,b),jnp.where(r==6,(t>=343).astype(F32),(r==7).astype(F32))).astype(BF)
    S['qmask'][...]=jnp.where(r<6,jnp.where(first,b,1.0-b),(r==6).astype(F32))*(-BIG)
    S['g1'][...]=g1[...]; S['g2'][...]=g2[...]
    wh=whead[...].astype(F32)
    S['wd'][...]=wh[:,1:2]-wh[:,0:1]
    for k in ('a_up','a_down','a_qkv','a_proj','a_head'): S[k][...]=jnp.zeros(S[k].shape,F32)
    for w in Ws:
        w['qblk'][...]=jnp.zeros((160,1152),BF)
        w['oblk'][...]=jnp.zeros((64,1152),BF)
        w['dkv'][...]=jnp.zeros((TL,256),BF)

def window(out, x, sign, act, S, W, wqkv, wproj, wup, wdown):
    x=x()
    g1=S['g1'][...]; g2=S['g2'][...]; wd=S['wd'][...]
    xh1,r1=norm(x)
    n1=(xh1*g1).astype(BF)
    yield
    packT=dot(S['qkvT'][...],n1).astype(BF)
    yield
    qT=packT[0:48]; kT=packT[48:96]; vT=packT[96:144]
    tok=dot(jnp.concatenate([n1,S['kmask'][...]],axis=0).T, S['wx'][...]).astype(BF)
    yield
    kaug=tok[:KP,0:160]; vaug=tok[:KP,256:320]; qtok=tok[:,384:432]
    qs=split3(qT.astype(F32)*LOG2E_4)
    r=lax.broadcasted_iota(jnp.int32,(16,1),0)
    sc=jnp.where(r<2,act[0],jnp.where(r<4,act[1],jnp.where(r<6,act[2],1.0)))
    qm=(S['qmask'][...]*sc).astype(BF)
    lane=lax.broadcasted_iota(jnp.int32,(1,C),1)
    for h in range(NH):
        ls=slice(h*TL,(h+1)*TL)
        for i in range(3):
            W['qblk'][48*i+16*h:48*i+16*h+16,ls]=qs[i][16*h:16*h+16]
        W['qblk'][144:160,ls]=qm
        hm=(lane>=16*h)&(lane<16*h+16)
        W['qt'][ls,:]=jnp.where(hm,qtok.astype(F32),0.0).astype(BF)
        yield
    mixp=[]
    vTk=vT[:,:KP]; kTk=kT[:,:KP]
    for a,b in CH:
        p=jnp.exp2(dot(kaug,W['qblk'][:,a:b]))
        yield
        inv=1.0/jnp.sum(p,axis=0,keepdims=True)
        P=(p*inv).astype(BF)
        W['P'][:,a:b]=P
        yield
        mixp.append(dot(vTk,P))
        yield
    mixa=jnp.concatenate(mixp,axis=1)
    mixf=jnp.concatenate([mixa[16*h:16*h+16,h*TL:(h+1)*TL] for h in range(NH)],axis=0)
    mixed=mixf.astype(BF)
    ao=dot(S['projT'][...],mixed).astype(BF).astype(F32)
    yield
    state=(x+ao).astype(BF).astype(F32)
    xh2,r2=norm(state)
    n2=(xh2*g2).astype(BF)
    yield
    hh=dot(S['upT'][...],n2)
    yield
    h2=hh*hh
    t=jnp.tanh(hh*(GC1+GC2*h2))
    s=0.5+0.5*t
    inf=hh*s
    inner=inf.astype(BF)
    dg=s+inf*(1.0-s)*(2*GC1+6*GC2*h2)
    yield
    res=(state+dot(S['downT'][...],inner)).astype(BF).astype(F32)
    yield
    z=jnp.sum(res*wd,axis=0,keepdims=True)
    g=sign*(1.0/(1.0+jnp.exp(-z*sign)))
    yield
    rg=res*g
    S['a_head'][...]+=rg[:,0:128]+rg[:,128:256]+rg[:,256:384]
    dres=(wd*g).astype(BF)
    dinner=dot(wdown[...],dres).astype(BF).astype(F32)
    yield
    S['a_down'][...]+=dot_t(dres,inner)
    yield
    dh=(dinner*dg).astype(BF)
    yield
    S['a_up'][...]+=dot_t(n2,dh)
    yield
    dn2=dot(wup[...],dh).astype(BF).astype(F32)
    yield
    dst=(dres.astype(F32)+norm_back(dn2*g2,xh2,r2)).astype(BF)
    yield
    S['a_proj'][...]+=dot_t(mixed,dst)
    dO=dot(wproj[...],dst).astype(BF)
    yield
    dOf=dO.astype(F32)
    dOtok=dO.T
    yield
    pr=mixf*dOf
    r16=lax.broadcasted_iota(jnp.int32,(16,TL),0)
    for h in range(NH):
        ls=slice(h*TL,(h+1)*TL)
        d=-jnp.sum(pr[16*h:16*h+16],axis=0,keepdims=True)
        d0,d1,d2=split3(d)
        W['oblk'][16*h:16*h+16,ls]=dO[16*h:16*h+16]
        W['oblk'][48:64,ls]=jnp.where(r16==0,d0.astype(F32),jnp.where(r16==1,d1.astype(F32),jnp.where(r16==2,d2.astype(F32),0.0))).astype(BF)
        hm=(lane>=16*h)&(lane<16*h+16)
        W['ot'][ls,:]=jnp.where(hm,dOtok.astype(F32),0.0).astype(BF)
        yield
    dqp=[]
    for a,b in CH:
        ds=W['P'][:,a:b]*dot(vaug,W['oblk'][:,a:b]).astype(BF)
        W['D'][:,a:b]=ds
        yield
        dqp.append(dot(kTk,ds))
        yield
    dqa=jnp.concatenate(dqp,axis=1)
    dq=(0.25*jnp.concatenate([dqa[16*h:16*h+16,h*TL:(h+1)*TL] for h in range(NH)],axis=0)).astype(BF)
    yield
    W['dkv'][0:KP,0:48]=(0.25*dot(W['D'][...],W['qt'][...])).astype(BF)
    yield
    W['dkv'][0:KP,128:176]=dot(W['P'][...],W['ot'][...]).astype(BF)
    yield
    dk=W['dkv'][:,0:128].T[0:48]; dv=W['dkv'][:,128:256].T[0:48]
    yield
    dpack=jnp.concatenate([dq,dk,dv],axis=0)
    S['a_qkv'][...]+=dot_t(n1,dpack)
    yield
    dn1=dot(wqkv[...],dpack).astype(BF).astype(F32)
    yield
    out((dst.astype(F32)+norm_back(dn1*g1,xh1,r1)).astype(BF))


def drive(gens, stagger=0):
    live=[]
    pend=list(gens); k=0
    while pend or live:
        if pend and (k>=stagger or not live):
            live.append(pend.pop(0)); k=0
            if stagger==0:
                live+=pend; pend=[]
        k+=1
        nxt=[]
        for g in live:
            try:
                next(g); nxt.append(g)
            except StopIteration: pass
        live=nxt


S_KEYS = tuple(scratch())
W_KEYS = tuple(win_scratch())


def comm_scratch(nx, ny):
    return dict(
        grid=pltpu.VMEM((WIN, 24, LW), F32),
        rows=pltpu.VMEM((NWY, 64, LW), F32),
        xs=pltpu.VMEM((NWY, 32, LW), BF),
        xr=pltpu.VMEM((NWY, 32, LW), BF),
        ys=pltpu.VMEM((16, LW), BF),
        yr=pltpu.VMEM((16, LW), BF),
        ds=pltpu.VMEM((16, LW), BF),
        dr=pltpu.VMEM((16, LW), BF),
        xwin=pltpu.VMEM((NZ, C, TL), BF),
        sg=pltpu.VMEM((8, TL), F32),
        zt=pltpu.VMEM((LAB, 128), BF),
        back=pltpu.VMEM((NWY, 64, WIDTH), F32),
        bxs=pltpu.VMEM((NWY, 32, WIDTH), BF),
        bxr=pltpu.VMEM((NWY, 32, WIDTH), BF),
        bys=pltpu.VMEM((16, WIDTH), BF),
        byr=pltpu.VMEM((16, WIDTH), BF),
        bds=pltpu.VMEM((16, WIDTH), BF),
        bdr=pltpu.VMEM((16, WIDTH), BF),
        tmp=pltpu.VMEM((64, WIDTH), F32),
        outf=pltpu.VMEM((WIN, 24, WIDTH), F32),
        part=pltpu.VMEM((nx, 256 // nx, 128), F32),
        r1=pltpu.VMEM((nx - 1, 256 // nx, 128), F32),
        csum=pltpu.VMEM((256 // nx, 128), F32),
        r2=pltpu.VMEM((ny - 1, 256 // nx, 128), F32),
        ctot=pltpu.VMEM((256 // nx, 128), F32),
        total=pltpu.VMEM((nx, 256 // nx, 128), F32),
        hs=pltpu.SemaphoreType.DMA((NWY + 2,)),
        hr=pltpu.SemaphoreType.DMA((NWY + 2,)),
        bs=pltpu.SemaphoreType.DMA((NWY + 2,)),
        br=pltpu.SemaphoreType.DMA((NWY + 2,)),
        s1=pltpu.SemaphoreType.DMA((nx - 1,)),
        q1=pltpu.SemaphoreType.DMA((nx - 1,)),
        s2=pltpu.SemaphoreType.DMA((ny - 1,)),
        q2=pltpu.SemaphoreType.DMA((ny - 1,)),
        s3=pltpu.SemaphoreType.DMA((nx - 1,)),
        q3=pltpu.SemaphoreType.DMA((nx - 1,)),
    )


def remote(src, dst, ssem, rsem, to):
    return pltpu.make_async_remote_copy(
        src_ref=src, dst_ref=dst, send_sem=ssem, recv_sem=rsem, device_id=to, device_id_type=MESH
    )


def make_kernel(nx, ny, tokens):
    c_keys = tuple(comm_scratch(nx, ny))

    def kernel(feat, lab, wqkv, wproj, wup, wdown, whead, g1, g2, *refs):
        out, o_qkv, o_proj, o_up, o_down, o_head = refs[:6]
        refs = refs[6:]
        S = dict(zip(S_KEYS, refs))
        refs = refs[len(S_KEYS):]
        Ws = [dict(zip(W_KEYS, refs[i * len(W_KEYS):])) for i in range(NZ)]
        Q = dict(zip(c_keys, refs[NZ * len(W_KEYS):]))
        mx = lax.axis_index("gx")
        my = lax.axis_index("gy")

        def at(dx, dy):
            return (lax.rem(mx + dx + nx, nx), lax.rem(my + dy + ny, ny))

        barrier = pltpu.get_barrier_semaphore()
        peers = [(k, 0) for k in range(1, nx)] + [(0, k) for k in range(1, ny)] + [(1, 1), (-1, -1)]
        for p in peers:
            pl.semaphore_signal(barrier, inc=1, device_id=at(*p), device_id_type=MESH)

        grid = Q["grid"]
        grid[:, 0:21, 0:WIDTH] = feat[...].astype(F32)
        grid[:, 0:21, WIDTH:LAB] = jnp.zeros((WIN, 21, LAB - WIDTH), F32)
        grid[:, 0:21, LAB:LW] = jnp.zeros((WIN, 21, LW - LAB), F32)
        grid[:, 0:21, LAB:LAB + DEPTH] = lab[...].astype(F32)
        tmp = Q["rows"]
        for wy in range(NWY):
            n = WIN if wy < 2 else 4
            for k in range(SHIFT):
                tmp[wy, 7 * k:7 * k + n, :] = grid[k, 7 * wy + 3:7 * wy + 3 + n, :]
            Q["xs"][wy] = tmp[wy, 0:32, :].astype(BF)
        for k in range(4):
            tmp[0, 3 * k:3 * k + 3, :] = grid[3 + k, 0:3, :]
        Q["ys"][...] = tmp[0, 0:16, :].astype(BF)
        for k in range(SHIFT):
            tmp[1, 3 * k:3 * k + 3, :] = grid[k, 0:3, :]
        Q["ds"][...] = tmp[1, 0:16, :].astype(BF)
        pl.semaphore_wait(barrier, len(peers))
        hs, hr = Q["hs"], Q["hr"]
        xcopy = [remote(Q["xs"].at[w], Q["xr"].at[w], hs.at[w], hr.at[w], at(-1, 0)) for w in range(NWY)]
        ycopy = remote(Q["ys"], Q["yr"], hs.at[3], hr.at[3], at(0, -1))
        dcopy = remote(Q["ds"], Q["dr"], hs.at[4], hr.at[4], at(-1, -1))
        xcopy[0].start()
        ycopy.start()
        dcopy.start()
        xcopy[1].start()
        xcopy[2].start()

        init(S, Ws, wqkv, wproj, wup, wdown, whead, g1, g2)
        rows = Q["rows"]
        for wy in range(NWY):
            n = WIN if wy < 2 else 4
            for k in range(4):
                rows[wy, 7 * k:7 * k + n, :] = grid[3 + k, 7 * wy + 3:7 * wy + 3 + n, :]
            rows[wy, 48:64, :] = jnp.zeros((16, LW), F32)
        Q["zt"][...] = jnp.zeros((LAB, 128), BF)

        act_x = (mx == nx - 1).astype(F32)
        last_y = my == ny - 1
        lanes = lax.broadcasted_iota(jnp.int32, (1, TL), 1)

        def step(wy, _):
            remote(Q["xs"].at[wy], Q["xr"].at[wy], hs.at[wy], hr.at[wy], at(-1, 0)).wait()
            rows[wy, 28:49, :] = Q["xr"][wy].astype(F32)[0:21]

            @pl.when(wy == 2)
            def _():
                ycopy.wait()
                dcopy.wait()
                Q["tmp"][0:16, :] = Q["yr"][:, 0:WIDTH].astype(F32)
                Q["tmp"][16:32, :] = Q["dr"][:, 0:WIDTH].astype(F32)
                yl = Q["yr"][:, LAB:LW].astype(F32)
                dl = Q["dr"][:, LAB:LW].astype(F32)
                for k in range(4):
                    rows[2, 7 * k + 4:7 * k + 7, 0:WIDTH] = Q["tmp"][3 * k:3 * k + 3, :]
                    rows[2, 7 * k + 4:7 * k + 7, LAB:LW] = yl[3 * k:3 * k + 3]
                for k in range(SHIFT):
                    rows[2, 28 + 7 * k + 4:28 + 7 * k + 7, 0:WIDTH] = Q["tmp"][16 + 3 * k:16 + 3 * k + 3, :]
                    rows[2, 28 + 7 * k + 4:28 + 7 * k + 7, LAB:LW] = dl[3 * k:3 * k + 3]

            cols = rows[wy].astype(BF).T
            for wz in range(NZ):
                zs = [(7 * wz + j + SHIFT) % DEPTH for j in range(WIN)]
                Q["xwin"][wz] = jnp.concatenate(
                    [cols[C * z:C * z + C, 0:49] for z in zs] + [jnp.zeros((C, TL - PT), BF)], axis=1
                )
                m = jnp.concatenate(
                    [cols[LAB + z:LAB + z + 1, 0:49].astype(F32) for z in zs] + [jnp.zeros((1, TL - PT), F32)],
                    axis=1,
                )
                Q["sg"][wz:wz + 1, :] = jnp.where(lanes < PT, 1.0 - 2.0 * m, 0.0)

            gens = []
            act_y = jnp.logical_and(last_y, wy == 2).astype(F32)
            for wz in range(NZ):
                def put(v, wz=wz):
                    for j in range(WIN):
                        z = (7 * wz + j + SHIFT) % DEPTH
                        Q["zt"][C * z:C * z + C, 0:49] = v[:, 49 * j:49 * j + 49]

                def get(wz=wz):
                    return Q["xwin"][wz].astype(F32)

                act = (act_x, act_y, F32(1.0 if wz == NZ - 1 else 0.0))
                gens.append(window(put, get, Q["sg"][wz:wz + 1, :], act, S, Ws[wz], wqkv, wproj, wup, wdown))
            drive(gens)
            flat = Q["zt"][...].T.astype(F32)[0:64, 0:WIDTH]
            Q["back"][wy] = flat
            Q["bxs"][wy] = jnp.concatenate([flat[28:49], jnp.zeros((11, WIDTH), F32)], axis=0).astype(BF)
            remote(Q["bxs"].at[wy], Q["bxr"].at[wy], Q["bs"].at[wy], Q["br"].at[wy], at(1, 0)).start()
            return 0

        lax.fori_loop(0, NWY, step, 0)

        a_head = jnp.sum(S["a_head"][...], axis=1, keepdims=True)
        acc = jnp.concatenate(
            [S["a_up"][...], S["a_down"][...], S["a_qkv"][...], S["a_proj"][...], a_head, jnp.zeros((C, 63), F32)],
            axis=1,
        )
        part = Q["part"]
        per = 256 // nx
        for j in range(16):
            if j < 15:
                v = acc[16 * (j % 3):16 * (j % 3) + 16, 128 * (j // 3):128 * (j // 3) + 128]
            else:
                v = jnp.zeros((16, 128), F32)
            part[j * 16 // per, (j * 16) % per:(j * 16) % per + 16, :] = v
        first = [
            remote(part.at[lax.rem(mx + k, nx)], Q["r1"].at[k - 1], Q["s1"].at[k - 1], Q["q1"].at[k - 1], at(k, 0))
            for k in range(1, nx)
        ]
        for c in first:
            c.start()

        back, tmp = Q["back"], Q["tmp"]
        for k in range(4):
            tmp[3 * k:3 * k + 3, :] = back[2, 7 * k + 4:7 * k + 7, :]
        for k in range(SHIFT):
            tmp[16 + 3 * k:16 + 3 * k + 3, :] = back[2, 28 + 7 * k + 4:28 + 7 * k + 7, :]
        Q["bys"][...] = tmp[0:16, :].astype(BF)
        Q["bds"][...] = tmp[16:32, :].astype(BF)
        bycopy = remote(Q["bys"], Q["byr"], Q["bs"].at[3], Q["br"].at[3], at(0, 1))
        bdcopy = remote(Q["bds"], Q["bdr"], Q["bs"].at[4], Q["br"].at[4], at(1, 1))
        bycopy.start()
        bdcopy.start()

        for c in first:
            c.wait()
        csum = part[mx]
        for k in range(nx - 1):
            csum = csum + Q["r1"][k]
        Q["csum"][...] = csum
        second = [
            remote(Q["csum"], Q["r2"].at[k - 1], Q["s2"].at[k - 1], Q["q2"].at[k - 1], at(0, k))
            for k in range(1, ny)
        ]
        for c in second:
            c.start()

        outf = Q["outf"]
        for x in range(SHIFT, WIN):
            k = x - SHIFT
            for wy in range(NWY):
                n = WIN if wy < 2 else 4
                outf[x, 7 * wy + 3:7 * wy + 3 + n, :] = back[wy, 7 * k:7 * k + n, :]

        for c in second:
            c.wait()
        order = csum
        for k in range(ny - 1):
            order = order + Q["r2"][k]
        Q["ctot"][...] = order * (1.0 / math.sqrt(tokens))
        Q["total"][mx] = Q["ctot"][...]
        third = [
            remote(Q["ctot"], Q["total"].at[mx], Q["s3"].at[k - 1], Q["q3"].at[k - 1], at(k, 0))
            for k in range(1, nx)
        ]
        for c in third:
            c.start()

        bycopy.wait()
        bdcopy.wait()
        tmp[0:16, :] = Q["byr"][...].astype(F32)
        tmp[16:32, :] = Q["bdr"][...].astype(F32)
        for k in range(4):
            outf[SHIFT + k, 0:3, :] = tmp[3 * k:3 * k + 3, :]
        for k in range(SHIFT):
            outf[k, 0:3, :] = tmp[16 + 3 * k:16 + 3 * k + 3, :]
        for wy in range(NWY):
            remote(Q["bxs"].at[wy], Q["bxr"].at[wy], Q["bs"].at[wy], Q["br"].at[wy], at(1, 0)).wait()
            n = WIN if wy < 2 else 4
            tmp[32:64, :] = Q["bxr"][wy].astype(F32)
            for k in range(SHIFT):
                outf[k, 7 * wy + 3:7 * wy + 3 + n, :] = tmp[32 + 7 * k:32 + 7 * k + n, :]
        out[...] = outf[:, 0:21, :].astype(BF)

        for c in third:
            c.wait()
        total = Q["total"]
        parts = []
        for l in range(5):
            parts.append(
                jnp.concatenate(
                    [total[j * 16 // per, (j * 16) % per:(j * 16) % per + 16, :] for j in range(3 * l, 3 * l + 3)],
                    axis=0,
                )
            )
        whole = jnp.concatenate(parts, axis=1)
        o_up[...] = whole[:, 0:192]
        o_down[...] = whole[:, 192:384]
        o_qkv[...] = whole[:, 384:528]
        o_proj[...] = whole[:, 528:576]
        o_head[...] = whole[:, 576:577]

    return kernel


def body(features, labels, gain_one, gain_two, w_qkv, w_proj, w_up, w_down, w_head):
    nx, ny = lax.axis_size("gx"), lax.axis_size("gy")
    tokens = nx * ny * features.shape[0] * features.shape[1] * DEPTH
    vmem = pl.BlockSpec(memory_space=pltpu.VMEM)
    shapes = [jax.ShapeDtypeStruct(features.shape, BF)] + [
        jax.ShapeDtypeStruct(s, F32) for s in ((C, 144), (C, C), (C, FF), (C, FF), (C, 1))
    ]
    back, d_qkv, d_proj, d_up, d_down, d_head = pl.pallas_call(
        make_kernel(nx, ny, tokens),
        out_shape=shapes,
        in_specs=[vmem] * 9,
        out_specs=[vmem] * 6,
        scratch_shapes=list(scratch().values())
        + list(win_scratch().values()) * NZ
        + list(comm_scratch(nx, ny).values()),
        compiler_params=pltpu.CompilerParams(
            collective_id=0, has_side_effects=True, vmem_limit_bytes=60 * 2**20
        ),
    )(
        features, labels, w_qkv, w_proj, w_up, w_down, w_head,
        gain_one.reshape(C, 1), gain_two.reshape(C, 1),
    )
    return back, d_qkv, d_proj, d_up, d_down.T, jnp.concatenate([-d_head, d_head], axis=1)


def solution(mesh):
    placed = (P("gx", "gy", None), P("gx", "gy", None), P(), P(), P(), P(), P(), P(), P())
    return jax.shard_map(
        body,
        mesh=mesh,
        in_specs=placed,
        out_specs=(P("gx", "gy", None), P(), P(), P(), P(), P()),
        check_vma=False,
    )
```

time: 452 us -> 82.9 us (0.18); the launches traced: 447 us -> 82.4 us
  waiting for transfers between devices: 183 us -> 0 us
  other arithmetic: 98.5 us -> 1.32 us
  matrix products: 77.3 us -> 0 us
  Pallas kernels: 0 us -> 69.7 us
  local copies, waits for them, and re-layouts: 53.9 us -> 10.7 us
  starting transfers between devices: 18.6 us -> 0 us
  between operations: 15.2 us -> 0.65 us
    psum x1 -> x0, waiting for transfers between devices: 137 us -> none  [body(): lax.psum((sums[0], sums[1], sums[2], sums[3], sums[4]), ('gx', 'gy'))]
    dot_general x54 -> x0, matrix products: 77.3 us -> none  [the longest x12 31.1 us: attend(): jnp.einsum('bphd,bqhd->bhpq', query, keys, preferred_element_type=jnp.flo...]
    pallas_call x0 -> x1, Pallas kernels: none -> 69.7 us  [body(): pl.pallas_call(make_kernel(nx, ny, tokens), out_shape=shapes, in_specs=[v...]
    ppermute x8 -> x0, waiting for transfers between devices: 45.7 us -> none  [passed_along(): lax.ppermute(x, axis, [(i, (i + by) % devices) for i in range(devices)])]
    convert_element_type x13 -> x0, other arithmetic: 42.5 us -> none  [the longest x6 25 us: attend(): (raw / jnp.sum(raw, axis=-1, keepdims=True)).astype(jnp.bfloat16)]
    reduce_sum x8 -> x0, other arithmetic: 24 us -> none  [the longest x2 8.85 us: layer_norm(): spread = values - centre]
    ppermute x8 -> x0, starting transfers between devices: 18.5 us -> none  [passed_along(): lax.ppermute(x, axis, [(i, (i + by) % devices) for i in range(devices)])]
    mul x10 -> x0, other arithmetic: 16.5 us -> none  [the longest x3 10.1 us: attend(): jnp.einsum('bphd,bqhd->bhpq', query, keys, preferred_element_type=jnp.flo...]
  transfers between devices with their start and end apart: 9 -> 0, of which waited for: 8 -> 0; matrix products, arithmetic and copies ran while one was open for 6% -> 0% of each run, Pallas kernels for 0% -> 0%
where the time goes in v1:
time: 82.9 us; the launch traced here: 82.4 us
  Pallas kernels  69.7 us (84%)
  local copies, waits for them, and re-layouts  10.7 us (13%)
  other arithmetic  1.32 us (2%)
    pallas_call x1, Pallas kernels, body(): pl.pallas_call(make_kernel(nx, ny, tokens), out_shape=shapes, in_specs=[v...  69.7 us
    unnamed x23, local copies, waits for them, and re-layouts  9.14 us

profile of v1, /device:TPU:1, one launch (start us, length us, event | category | flops | bytes accessed | tf_op | source)
XLA Modules:
  0.0 82.4 jit_solution(132004261371809678)
XLA Ops:
  0.6 1.5 %copy.20.wdown = bf16[192,48]{1,0:T(8,128)(2,1)} copy(bf16[192,48]{0,1:T(8,128)(2,1)} %param.16) | data formatting | bytes 36864 | tf_op args[7]
  2.1 0.0 copy-start.5
  2.1 0.7 copy-done.5
  2.7 0.7 copy.22.g1
  3.4 0.0 copy-start.6
  3.4 0.7 copy-done.6
  4.1 0.0 copy-start.7
  4.1 0.7 copy.23.g2
  4.8 0.0 copy-done.7
  4.8 0.7 copy.21.whead
  5.5 69.7 %shard_map.136 = (bf16[7,21,2016]{2,1,0:T(8,128)(2,1)}, f32[48,144]{1,0:T(8,128)}, f32[48,48]{1,0:T(8,128)}, f32[48,192]{1,0:T(8,128)}, f32[48,192]{1,0:T(8,128)}, /*index=5*/f32[48,1]{1,0:T(8,128)}) custom-call(bf16[7,21,2016]{2,1,0:T(8,128)(2,1)} %feat.1, s32[7,21,42]{2,1,0:T(8,128)} %lab.1, bf16[48,144]{1,0:T(8,128)(2,1)} %wqkv.1, bf16[48,48]{1,0:T(8,128)(2,1)} %wproj.1, ...), custom_call_target="tpu_custom_call" | custom-call | tf_op jit(solution)/shard_map/pallas_call | solution.py:497
  75.2 0.7 neg.3
  76.0 0.0 copy-start
  76.0 0.1 copy.24
  76.1 0.7 copy-done
  76.7 0.1 copy.25
  76.8 0.6 pad_maximum_fusion
  77.4 0.0 copy-start.3
  77.4 2.0 %copy.31 = bf16[7,21,2016]{2,1,0:T(8,128)(2,1)} copy(bf16[7,21,2016]{2,1,0:T(8,128)(2,1)} %get-tuple-element.30) | data formatting | bytes 1185408
  79.4 0.0 copy-done.3
  79.4 0.0 copy-start.4
  79.4 0.6 copy.32
  80.0 0.1 copy-done.4
  80.1 0.0 copy-start.2
  80.1 0.6 copy.33
  80.8 0.2 copy-done.2
  81.0 0.0 copy-start.1
  81.0 0.6 copy.34
  81.6 0.2 copy-done.1
  81.8 0.6 copy.35
Async XLA Ops:
  2.1 0.7 copy-start.5
  3.4 0.7 copy-start.6
  4.1 0.7 copy-start.7
  76.0 0.7 copy-start
  77.4 2.0 %copy-start.3 = (f32[48,144]{1,0:T(8,128)S(1)}, f32[48,144]{1,0:T(8,128)}, u32[]{:S(2)}) copy-start(f32[48,144]{1,0:T(8,128)} %get-tuple-element.31) | copy-start | bytes 82948
  79.4 0.7 copy-start.4
  80.1 0.8 copy-start.2
  81.0 0.8 copy-start.1

commit v2 on v1

v2 whole, which is shorter than its diff:
```python
import math

import jax
import jax.numpy as jnp
from jax import lax
from jax.experimental import pallas as pl
from jax.experimental.pallas import tpu as pltpu
from jax.sharding import PartitionSpec as P

BF = jnp.bfloat16
F32 = jnp.float32
C = 48
FF = 192
NH = 3
WIN = 7
SHIFT = 3
DEPTH = 42
WIDTH = DEPTH * C
LAB = 2048
LW = 2176
KP = 352
TL = 384
PT = 343
NZ = 6
NWY = 3
EPS = 1e-5
BIG = 2.0**100
LOG2E_4 = 0.25 * math.log2(math.e)
CH = [(0, 256), (256, 512), (512, 768), (768, 1024), (1024, 1152)]
GC1 = math.sqrt(2 / math.pi)
GC2 = 0.044715 * GC1
MESH = pl.DeviceIdType.MESH


def dot(a,b): return lax.dot_general(a,b,(((1,),(0,)),((),())),preferred_element_type=F32)
def dot_t(a,b): return lax.dot_general(a,b,(((1,),(1,)),((),())),preferred_element_type=F32)
def split3(v):
    a=v.astype(BF); r=v-a.astype(F32); b=r.astype(BF); r=r-b.astype(F32); return a,b,r.astype(BF)
def mean0(v): return jnp.sum(v,axis=0,keepdims=True)*(1.0/C)
def norm(v):
    s=v-mean0(v)
    r=lax.rsqrt(mean0(s*s)+EPS)
    return s*r, r
def norm_back(d,xh,r):
    return (d-mean0(d)-xh*mean0(d*xh))*r

def scratch():
    return dict(
      qkvT=pltpu.VMEM((144,C),BF), projT=pltpu.VMEM((C,C),BF), upT=pltpu.VMEM((FF,C),BF), downT=pltpu.VMEM((C,FF),BF), down=pltpu.VMEM((FF,C),BF),
      wx=pltpu.VMEM((128,512),BF), kmask=pltpu.VMEM((16,TL),BF), qmask=pltpu.VMEM((16,TL),F32),
      g1=pltpu.VMEM((C,1),F32), g2=pltpu.VMEM((C,1),F32), wd=pltpu.VMEM((C,1),F32),
      a_up=pltpu.VMEM((C,FF),F32), a_down=pltpu.VMEM((C,FF),F32), a_qkv=pltpu.VMEM((C,144),F32), a_proj=pltpu.VMEM((C,C),F32), a_head=pltpu.VMEM((C,128),F32),
    )
def win_scratch():
    return dict(qblk=pltpu.VMEM((240,2304),BF), oblk=pltpu.VMEM((256,2304),BF), P=pltpu.VMEM((KP,2304),BF), D=pltpu.VMEM((KP,2304),BF),
       qt=pltpu.VMEM((2304,128),BF), ot=pltpu.VMEM((2304,128),BF), dkv=pltpu.VMEM((TL,256),BF))

def init(S, Ws, wqkv, wproj, wup, wdownT, whT, g1, g2):
    S['qkvT'][...]=wqkv[...].T
    S['projT'][...]=wproj[...].T
    S['upT'][...]=wup[...].T
    S['downT'][...]=wdownT[...]
    S['down'][...]=wdownT[...].T
    wq=wqkv[...].astype(F32)
    wk=wq[:,48:96]; wv=wq[:,96:144]
    z=lambda n: jnp.zeros((C,n),F32)
    r=lax.broadcasted_iota(jnp.int32,(16,512),0); l=lax.broadcasted_iota(jnp.int32,(16,512),1)
    wqq=wq[:,0:48]
    rows_a=jnp.concatenate([wk,wk,z(160),wv,z(16),wqq,z(144)],axis=1)
    mask_a=((l==96+r)|((l>=304)&(l<307)&(r==7))).astype(F32)
    rows_b=jnp.concatenate([z(128),wk,wk,z(160),wqq,z(16),wv,z(16)],axis=1)
    mask_b=((l==224+r)|((l>=496)&(l<499)&(r==7))).astype(F32)
    S['wx'][...]=jnp.concatenate([rows_a,mask_a,rows_b,mask_b],axis=0).astype(BF)
    t=lax.broadcasted_iota(jnp.int32,(16,TL),1); r=lax.broadcasted_iota(jnp.int32,(16,TL),0)
    bz=(t>=4*49).astype(F32)
    u=t-49*sum((t>=49*k).astype(jnp.int32) for k in range(1,7))
    bx=(u>=28).astype(F32)
    v=u-7*sum((u>=7*k).astype(jnp.int32) for k in range(1,7))
    by=(v>=4).astype(F32)
    b=jnp.where(r<2,bx,jnp.where(r<4,by,bz))
    first=(r%2)==0
    S['kmask'][...]=jnp.where(r<6,jnp.where(first,1.0-b,b),jnp.where(r==6,(t>=343).astype(F32),(r==7).astype(F32))).astype(BF)
    S['qmask'][...]=jnp.where(r<6,jnp.where(first,b,1.0-b),(r==6).astype(F32))*(-BIG)
    wh=whT[...].astype(F32)
    cols=jnp.concatenate([g1[...],g2[...],wh[1:2]-wh[0:1],jnp.zeros((5,C),F32)],axis=0)
    cols=jnp.concatenate([cols,jnp.zeros((8,128-C),F32)],axis=1).T
    S['g1'][...]=cols[0:C,0:1]; S['g2'][...]=cols[0:C,1:2]; S['wd'][...]=cols[0:C,2:3]
    for k in ('a_up','a_down','a_qkv','a_proj','a_head'): S[k][...]=jnp.zeros(S[k].shape,F32)
    for w in Ws:
        w['qblk'][...]=jnp.zeros((240,2304),BF)
        w['oblk'][...]=jnp.zeros((256,2304),BF)
        w['dkv'][...]=jnp.zeros((TL,256),BF)

def split2(v):
    a=v.astype(BF); return a,(v-a.astype(F32)).astype(BF)

def spread(parts):
    def block(j):
        c=j//2; k0=256*c//TL; k=j//3
        return parts[c][16*(k-k0):16*(k-k0)+16,128*(j%2):128*(j%2)+128]
    cols=[jnp.concatenate([block(3*k+i) for i in range(3)],axis=1) for k in range(6)]
    return jnp.concatenate([jnp.concatenate(cols[0:3],axis=0),jnp.concatenate(cols[3:6],axis=0)],axis=1)

def heads_of(c):
    return slice(16*(256*c//TL),16*((256*c+255)//TL)+16)

def window(out, x, sign, act, S, W, wqkv, wproj, wup):
    x=x()
    g1=S['g1'][...]; g2=S['g2'][...]; wd=S['wd'][...]
    n1=(norm(x)[0]*g1).astype(BF)
    yield
    packT=dot(S['qkvT'][...],n1).astype(BF)
    yield
    km=S['kmask'][...]
    tok=dot(jnp.concatenate([n1[:,0:TL],km,n1[:,TL:],km],axis=0).T, S['wx'][...]).astype(BF)
    yield
    qs=split2(packT[0:48].astype(F32)*LOG2E_4)
    r=lax.broadcasted_iota(jnp.int32,(16,1),0)
    lane=lax.broadcasted_iota(jnp.int32,(1,128),1)
    for w in range(2):
        sc=jnp.where(r<2,act[0],jnp.where(r<4,act[1],jnp.where(r<6,act[2+w],1.0)))
        qm=(S['qmask'][...]*sc).astype(BF)
        qtok=tok[:,256+128*w:384+128*w].astype(F32)
        for h in range(NH):
            k=3*w+h; ls=slice(k*TL,(k+1)*TL)
            for i in range(2):
                W['qblk'][128*w+48*i+16*h:128*w+48*i+16*h+16,ls]=qs[i][16*h:16*h+16,TL*w:TL*w+TL]
            W['qblk'][128*w+96:128*w+112,ls]=qm
            l0=64*(1-w)+16*h
            W['qt'][ls,:]=jnp.where((lane>=l0)&(lane<l0+16),qtok,0.0).astype(BF)
            yield
    tk=tok[:KP]
    vT=jnp.concatenate([packT[96:144,0:KP],packT[96:144,TL:TL+KP]],axis=0)
    kT=jnp.concatenate([packT[48:96,0:KP],packT[48:96,TL:TL+KP]],axis=0)
    def fwd_dot(c):
        rs=slice(0,112) if c<4 else (slice(0,240) if c==4 else slice(128,240))
        return jnp.exp2(dot(tk[:,rs],W['qblk'][rs,256*c:256*c+256]))
    mixp=[]
    p=fwd_dot(0)
    for c in range(9):
        yield
        nxt=fwd_dot(c+1) if c<8 else None
        P=(p*(1.0/jnp.sum(p,axis=0,keepdims=True))).astype(BF)
        W['P'][:,256*c:256*c+256]=P
        yield
        mixp.append(dot(vT[heads_of(c)],P))
        p=nxt
    mixf=spread(mixp)
    mixed=mixf.astype(BF)
    ao=dot(S['projT'][...],mixed).astype(BF).astype(F32)
    yield
    state=(x+ao).astype(BF).astype(F32)
    xh2,r2=norm(state)
    n2=(xh2*g2).astype(BF)
    yield
    hh=dot(S['upT'][...],n2)
    yield
    h2=hh*hh
    t=jnp.tanh(hh*(GC1+GC2*h2))
    s=0.5+0.5*t
    inf=hh*s
    inner=inf.astype(BF)
    dg=s+inf*(1.0-s)*(2*GC1+6*GC2*h2)
    yield
    res=(state+dot(S['downT'][...],inner)).astype(BF).astype(F32)
    yield
    z=jnp.sum(res*wd,axis=0,keepdims=True)
    g=sign*(1.0/(1.0+jnp.exp(-z*sign)))
    rg=res*g
    S['a_head'][...]+=sum(rg[:,128*i:128*i+128] for i in range(1,6))+rg[:,0:128]
    dres=(wd*g).astype(BF)
    yield
    dinner=dot(S['down'][...],dres).astype(BF).astype(F32)
    yield
    S['a_down'][...]+=dot_t(dres,inner)
    yield
    dh=(dinner*dg).astype(BF)
    yield
    S['a_up'][...]+=dot_t(n2,dh)
    yield
    dn2=dot(wup[...],dh).astype(BF).astype(F32)
    yield
    dst=(dres.astype(F32)+norm_back(dn2*g2,xh2,r2)).astype(BF)
    yield
    S['a_proj'][...]+=dot_t(mixed,dst)
    yield
    dO=dot(wproj[...],dst).astype(BF)
    yield
    zr=jnp.zeros((16,TL),BF)
    dOtok=jnp.concatenate([dO[:,TL:],zr,dO[:,0:TL],zr],axis=0).T.astype(F32)
    yield
    pr=mixf*dO.astype(F32)
    r16=lax.broadcasted_iota(jnp.int32,(16,TL),0)
    for w in range(2):
        for h in range(NH):
            k=3*w+h; ls=slice(k*TL,(k+1)*TL); ws=slice(TL*w,TL*w+TL); o=192*w
            d0,d1,d2=split3(-jnp.sum(pr[16*h:16*h+16,ws],axis=0,keepdims=True))
            W['oblk'][o+16*h:o+16*h+16,ls]=dO[16*h:16*h+16,ws]
            W['oblk'][o+48:o+64,ls]=jnp.where(r16==0,d0.astype(F32),jnp.where(r16==1,d1.astype(F32),jnp.where(r16==2,d2.astype(F32),0.0))).astype(BF)
            l0=64*(1-w)+16*h
            W['ot'][ls,:]=jnp.where((lane>=l0)&(lane<l0+16),dOtok,0.0).astype(BF)
            yield
    def bwd_dot(c):
        rs=slice(0,64) if c<4 else (slice(0,256) if c==4 else slice(128,256))
        return dot(tk[:,rs.start+256:rs.stop+256],W['oblk'][rs,256*c:256*c+256]).astype(BF)
    dqp=[]
    dp=bwd_dot(0)
    for c in range(9):
        yield
        nxt=bwd_dot(c+1) if c<8 else None
        cs=slice(256*c,256*c+256)
        ds=W['P'][:,cs]*dp
        W['D'][:,cs]=ds
        yield
        dqp.append(dot(kT[heads_of(c)],ds))
        dp=nxt
    dq=(0.25*spread(dqp)).astype(BF)
    yield
    W['dkv'][0:KP,128:256]=dot(W['P'][...],W['ot'][...]).astype(BF)
    yield
    W['dkv'][0:KP,0:128]=(0.25*dot(W['D'][...],W['qt'][...])).astype(BF)
    yield
    dk=W['dkv'][:,0:128].T; dv=W['dkv'][:,128:256].T
    dpack=jnp.concatenate([dq,jnp.concatenate([dk[64:112],dk[0:48]],axis=1),jnp.concatenate([dv[64:112],dv[0:48]],axis=1)],axis=0)
    yield
    S['a_qkv'][...]+=dot_t(n1,dpack)
    out(dpack,dst)

def finish(x, dpack, dst, S, wqkv):
    g1=S['g1'][...]
    xh1,r1=norm(x)
    dn1=dot(wqkv[...],dpack).astype(BF).astype(F32)
    return (dst.astype(F32)+norm_back(dn1*g1,xh1,r1)).astype(BF)


def drive(gens, stagger=0):
    live=[]
    pend=list(gens); k=0
    while pend or live:
        if pend and (k>=stagger or not live):
            live.append(pend.pop(0)); k=0
            if stagger==0:
                live+=pend; pend=[]
        k+=1
        nxt=[]
        for g in live:
            try:
                next(g); nxt.append(g)
            except StopIteration: pass
        live=nxt


G1 = 8
G2 = 16
ROWS = 32
NP = 3
S_KEYS = tuple(scratch())
W_KEYS = tuple(win_scratch())


def comm_scratch(nx, ny):
    return dict(
        grid=pltpu.VMEM((WIN, 24, LW), F32),
        rows=pltpu.VMEM((NWY, 64, LW), F32),
        xs=pltpu.VMEM((NWY, 32, LW), BF),
        xr=pltpu.VMEM((NWY, 32, LW), BF),
        ys=pltpu.VMEM((16, LW), BF),
        yr=pltpu.VMEM((16, LW), BF),
        ds=pltpu.VMEM((16, LW), BF),
        dr=pltpu.VMEM((16, LW), BF),
        xwin=pltpu.VMEM((NWY * NP, C, 2 * TL), BF),
        dpk=pltpu.VMEM((NWY * NP, 3 * C, 2 * TL), BF),
        dst=pltpu.VMEM((NWY * NP, C, 2 * TL), BF),
        sg=pltpu.VMEM((8, 2 * TL), F32),
        zt=pltpu.VMEM((LAB, 128), BF),
        back=pltpu.VMEM((NWY, 64, WIDTH), F32),
        bxs=pltpu.VMEM((NWY, 32, WIDTH), BF),
        bxr=pltpu.VMEM((NWY, 32, WIDTH), BF),
        bys=pltpu.VMEM((16, WIDTH), BF),
        byr=pltpu.VMEM((16, WIDTH), BF),
        bds=pltpu.VMEM((16, WIDTH), BF),
        bdr=pltpu.VMEM((16, WIDTH), BF),
        tmp=pltpu.VMEM((64, WIDTH), F32),
        outf=pltpu.VMEM((WIN, 24, WIDTH), F32),
        part=pltpu.VMEM((G1, ROWS, 128), F32),
        r1=pltpu.VMEM((G1 - 1, ROWS, 128), F32),
        r2=pltpu.VMEM((G2, ROWS, 128), BF),
        total=pltpu.VMEM((G1, ROWS, 128), F32),
        hs=pltpu.SemaphoreType.DMA((NWY + 2,)),
        hr=pltpu.SemaphoreType.DMA((NWY + 2,)),
        bs=pltpu.SemaphoreType.DMA((NWY + 2,)),
        br=pltpu.SemaphoreType.DMA((NWY + 2,)),
        s1=pltpu.SemaphoreType.DMA((G1 - 1,)),
        q1=pltpu.SemaphoreType.DMA((G1 - 1,)),
        s2=pltpu.SemaphoreType.DMA((G2 - 1,)),
        q2=pltpu.SemaphoreType.DMA((G2 - 1,)),
        s3=pltpu.SemaphoreType.DMA((G1 - 1,)),
        q3=pltpu.SemaphoreType.DMA((G1 - 1,)),
    )


def remote(src, dst, ssem, rsem, to):
    return pltpu.make_async_remote_copy(
        src_ref=src, dst_ref=dst, send_sem=ssem, recv_sem=rsem, device_id=to, device_id_type=MESH
    )


def make_kernel(nx, ny, tokens):
    c_keys = tuple(comm_scratch(nx, ny))

    def kernel(feat, lab, wqkv, wproj, wup, wdown, whead, g1, g2, *refs):
        out, o_sum = refs[:2]
        refs = refs[2:]
        S = dict(zip(S_KEYS, refs))
        refs = refs[len(S_KEYS):]
        Ws = [dict(zip(W_KEYS, refs[i * len(W_KEYS):])) for i in range(NP)]
        Q = dict(zip(c_keys, refs[NP * len(W_KEYS):]))
        mx = lax.axis_index("gx")
        my = lax.axis_index("gy")

        def at(dx, dy):
            return (lax.rem(mx + dx + nx, nx), lax.rem(my + dy + ny, ny))

        half = lax.rem(lax.div(mx, 2), 2)
        core = lax.rem(mx, 2)
        px = lax.div(mx, 4)
        m1 = px * 2 + core
        m2 = half * ny + my

        def in_one(k):
            x2 = lax.rem(px + k // 2, 4)
            c2 = lax.rem(core + k % 2, 2)
            return x2 * 2 + c2, ((x2 * 2 + half) * 2 + c2, my)

        def in_two(k):
            h2 = lax.rem(half + k // ny, 2)
            return ((px * 2 + h2) * 2 + core, lax.rem(my + k % ny, ny))

        barrier = pltpu.get_barrier_semaphore()
        peers = [at(1, 0), at(-1, 0), at(1, 1), at(-1, -1)]
        peers += [in_one(k)[1] for k in range(1, G1)] + [in_two(k) for k in range(1, G2)]
        for p in peers:
            pl.semaphore_signal(barrier, inc=1, device_id=p, device_id_type=MESH)

        grid = Q["grid"]
        grid[:, 0:21, 0:WIDTH] = feat[...].astype(F32)
        grid[:, 0:21, WIDTH:LAB] = jnp.zeros((WIN, 21, LAB - WIDTH), F32)
        grid[:, 0:21, LAB:LW] = jnp.zeros((WIN, 21, LW - LAB), F32)
        grid[:, 0:21, LAB:LAB + DEPTH] = lab[...].astype(F32)
        tmp = Q["rows"]
        for wy in range(NWY):
            n = WIN if wy < 2 else 4
            for k in range(SHIFT):
                tmp[wy, 7 * k:7 * k + n, :] = grid[k, 7 * wy + 3:7 * wy + 3 + n, :]
            Q["xs"][wy] = tmp[wy, 0:32, :].astype(BF)
        for k in range(4):
            tmp[0, 3 * k:3 * k + 3, :] = grid[3 + k, 0:3, :]
        Q["ys"][...] = tmp[0, 0:16, :].astype(BF)
        for k in range(SHIFT):
            tmp[1, 3 * k:3 * k + 3, :] = grid[k, 0:3, :]
        Q["ds"][...] = tmp[1, 0:16, :].astype(BF)
        pl.semaphore_wait(barrier, len(peers))
        hs, hr = Q["hs"], Q["hr"]
        xcopy = [remote(Q["xs"].at[w], Q["xr"].at[w], hs.at[w], hr.at[w], at(-1, 0)) for w in range(NWY)]
        ycopy = remote(Q["ys"], Q["yr"], hs.at[3], hr.at[3], at(0, -1))
        dcopy = remote(Q["ds"], Q["dr"], hs.at[4], hr.at[4], at(-1, -1))
        xcopy[0].start()
        ycopy.start()
        dcopy.start()
        xcopy[1].start()
        xcopy[2].start()

        init(S, Ws, wqkv, wproj, wup, wdown, whead, g1, g2)
        rows = Q["rows"]
        for wy in range(NWY):
            n = WIN if wy < 2 else 4
            for k in range(4):
                rows[wy, 7 * k:7 * k + n, :] = grid[3 + k, 7 * wy + 3:7 * wy + 3 + n, :]
            rows[wy, 48:64, :] = jnp.zeros((16, LW), F32)
        Q["zt"][...] = jnp.zeros((LAB, 128), BF)

        act_x = (mx == nx - 1).astype(F32)
        last_y = my == ny - 1
        lanes = lax.broadcasted_iota(jnp.int32, (1, TL), 1)

        def step(wy, _):
            remote(Q["xs"].at[wy], Q["xr"].at[wy], hs.at[wy], hr.at[wy], at(-1, 0)).wait()
            rows[wy, 28:49, :] = Q["xr"][wy].astype(F32)[0:21]

            @pl.when(wy == 2)
            def _():
                ycopy.wait()
                dcopy.wait()
                Q["tmp"][0:16, :] = Q["yr"][:, 0:WIDTH].astype(F32)
                Q["tmp"][16:32, :] = Q["dr"][:, 0:WIDTH].astype(F32)
                yl = Q["yr"][:, LAB:LW].astype(F32)
                dl = Q["dr"][:, LAB:LW].astype(F32)
                for k in range(4):
                    rows[2, 7 * k + 4:7 * k + 7, 0:WIDTH] = Q["tmp"][3 * k:3 * k + 3, :]
                    rows[2, 7 * k + 4:7 * k + 7, LAB:LW] = yl[3 * k:3 * k + 3]
                for k in range(SHIFT):
                    rows[2, 28 + 7 * k + 4:28 + 7 * k + 7, 0:WIDTH] = Q["tmp"][16 + 3 * k:16 + 3 * k + 3, :]
                    rows[2, 28 + 7 * k + 4:28 + 7 * k + 7, LAB:LW] = dl[3 * k:3 * k + 3]

            cols = rows[wy].astype(BF).T
            zero = jnp.zeros((C, TL - PT), BF)
            zrow = jnp.zeros((1, TL - PT), F32)
            for p in range(NP):
                zs = [[(7 * wz + j + SHIFT) % DEPTH for j in range(WIN)] for wz in (2 * p, 2 * p + 1)]
                halves = [jnp.concatenate([cols[C * z:C * z + C, 0:49] for z in w] + [zero], axis=1) for w in zs]
                Q["xwin"][NP * wy + p] = jnp.concatenate(halves, axis=1)
                marks = [
                    jnp.concatenate([cols[LAB + z:LAB + z + 1, 0:49].astype(F32) for z in w] + [zrow], axis=1)
                    for w in zs
                ]
                Q["sg"][p:p + 1, :] = jnp.concatenate(
                    [jnp.where(lanes < PT, 1.0 - 2.0 * m, 0.0) for m in marks], axis=1
                )

            gens = []
            act_y = jnp.logical_and(last_y, wy == 2).astype(F32)
            for p in range(NP):
                def put(dpack, dst, p=p):
                    Q["dpk"][NP * wy + p] = dpack
                    Q["dst"][NP * wy + p] = dst

                def get(p=p):
                    return Q["xwin"][NP * wy + p].astype(F32)

                act = (act_x, act_y, F32(0.0), F32(1.0 if p == NP - 1 else 0.0))
                gens.append(window(put, get, Q["sg"][p:p + 1, :], act, S, Ws[p], wqkv, wproj, wup))
            drive(gens, 1)
            return 0

        lax.fori_loop(0, NWY, step, 0)

        a_head = jnp.sum(S["a_head"][...], axis=1, keepdims=True)
        acc = jnp.concatenate(
            [S["a_up"][...], S["a_down"][...], S["a_qkv"][...], S["a_proj"][...], a_head, jnp.zeros((C, 63), F32)],
            axis=1,
        )
        part = Q["part"]
        for j in range(16):
            if j < 15:
                v = acc[16 * (j % 3):16 * (j % 3) + 16, 128 * (j // 3):128 * (j // 3) + 128]
            else:
                v = jnp.zeros((16, 128), F32)
            part[j // 2, 16 * (j % 2):16 * (j % 2) + 16, :] = v
        first = []
        for k in range(1, G1):
            slot, to = in_one(k)
            first.append(remote(part.at[slot], Q["r1"].at[k - 1], Q["s1"].at[k - 1], Q["q1"].at[k - 1], to))
        for c in first:
            c.start()

        def tail(wy):
            for p in range(NP):
                v = finish(Q["xwin"][NP * wy + p].astype(F32), Q["dpk"][NP * wy + p], Q["dst"][NP * wy + p], S, wqkv)
                for i in range(2):
                    for j in range(WIN):
                        z = (7 * (2 * p + i) + j + SHIFT) % DEPTH
                        Q["zt"][C * z:C * z + C, 0:49] = v[:, TL * i + 49 * j:TL * i + 49 * j + 49]
            flat = Q["zt"][...].T.astype(F32)[0:64, 0:WIDTH]
            Q["back"][wy] = flat
            Q["bxs"][wy] = jnp.concatenate([flat[28:49], jnp.zeros((11, WIDTH), F32)], axis=0).astype(BF)
            remote(Q["bxs"].at[wy], Q["bxr"].at[wy], Q["bs"].at[wy], Q["br"].at[wy], at(1, 0)).start()

        tail(2)
        back, tmp = Q["back"], Q["tmp"]
        for k in range(4):
            tmp[3 * k:3 * k + 3, :] = back[2, 7 * k + 4:7 * k + 7, :]
        for k in range(SHIFT):
            tmp[16 + 3 * k:16 + 3 * k + 3, :] = back[2, 28 + 7 * k + 4:28 + 7 * k + 7, :]
        Q["bys"][...] = tmp[0:16, :].astype(BF)
        Q["bds"][...] = tmp[16:32, :].astype(BF)
        bycopy = remote(Q["bys"], Q["byr"], Q["bs"].at[3], Q["br"].at[3], at(0, 1))
        bdcopy = remote(Q["bds"], Q["bdr"], Q["bs"].at[4], Q["br"].at[4], at(1, 1))
        bycopy.start()
        bdcopy.start()

        for c in first:
            c.wait()
        csum = part[m1]
        for k in range(G1 - 1):
            csum = csum + Q["r1"][k]
        r2 = Q["r2"]
        r2[m2] = csum.astype(BF)
        second = [
            remote(r2.at[m2], r2.at[m2], Q["s2"].at[k - 1], Q["q2"].at[k - 1], in_two(k)) for k in range(1, G2)
        ]
        for c in second:
            c.start()

        tail(0)
        tail(1)

        outf = Q["outf"]
        for x in range(SHIFT, WIN):
            k = x - SHIFT
            for wy in range(NWY):
                n = WIN if wy < 2 else 4
                outf[x, 7 * wy + 3:7 * wy + 3 + n, :] = back[wy, 7 * k:7 * k + n, :]

        for c in second:
            c.wait()
        ctot = r2[0].astype(F32)
        for k in range(1, G2):
            ctot = ctot + r2[k].astype(F32)
        total = Q["total"]
        total[m1] = ctot * (1.0 / math.sqrt(tokens))
        third = [
            remote(total.at[m1], total.at[m1], Q["s3"].at[k - 1], Q["q3"].at[k - 1], in_one(k)[1])
            for k in range(1, G1)
        ]
        for c in third:
            c.start()

        bycopy.wait()
        bdcopy.wait()
        tmp[0:16, :] = Q["byr"][...].astype(F32)
        tmp[16:32, :] = Q["bdr"][...].astype(F32)
        for k in range(4):
            outf[SHIFT + k, 0:3, :] = tmp[3 * k:3 * k + 3, :]
        for k in range(SHIFT):
            outf[k, 0:3, :] = tmp[16 + 3 * k:16 + 3 * k + 3, :]
        for wy in range(NWY):
            remote(Q["bxs"].at[wy], Q["bxr"].at[wy], Q["bs"].at[wy], Q["br"].at[wy], at(1, 0)).wait()
            n = WIN if wy < 2 else 4
            tmp[32:64, :] = Q["bxr"][wy].astype(F32)
            for k in range(SHIFT):
                outf[k, 7 * wy + 3:7 * wy + 3 + n, :] = tmp[32 + 7 * k:32 + 7 * k + n, :]
        out[...] = outf[:, 0:21, :].astype(BF)

        for c in third:
            c.wait()
        parts = []
        for l in range(5):
            parts.append(
                jnp.concatenate(
                    [total[j // 2, 16 * (j % 2):16 * (j % 2) + 16, :] for j in range(3 * l, 3 * l + 3)], axis=0
                )
            )
        whole = jnp.concatenate(parts, axis=1)
        o_sum[...] = whole

    return kernel


def deliver(back, sums, out, o_qkv, o_proj, o_up, o_down, o_head):
    out[...] = back[...]
    o_up[...] = sums[:, 0:192]
    o_down[...] = sums[:, 192:384]
    o_qkv[...] = sums[:, 384:528]
    o_proj[...] = sums[:, 528:576]
    col = sums[:, 512:640].T[64:65]
    o_head[...] = jnp.concatenate([-col, col], axis=0)


def body(features, labels, gain_one, gain_two, w_qkv, w_proj, w_up, w_down, w_head):
    nx, ny = lax.axis_size("gx"), lax.axis_size("gy")
    tokens = nx * ny * features.shape[0] * features.shape[1] * DEPTH
    vmem = pl.BlockSpec(memory_space=pltpu.VMEM)
    back, sums = pl.pallas_call(
        make_kernel(nx, ny, tokens),
        out_shape=[jax.ShapeDtypeStruct(features.shape, BF), jax.ShapeDtypeStruct((C, 640), F32)],
        in_specs=[vmem] * 9,
        out_specs=[vmem] * 2,
        scratch_shapes=list(scratch().values())
        + list(win_scratch().values()) * NP
        + list(comm_scratch(nx, ny).values()),
        compiler_params=pltpu.CompilerParams(
            collective_id=0, has_side_effects=True, vmem_limit_bytes=60 * 2**20
        ),
    )(
        features, labels, w_qkv, w_proj, w_up, w_down.T, w_head.T,
        gain_one.reshape(1, C), gain_two.reshape(1, C),
    )
    out, d_qkv, d_proj, d_up, d_down, d_head = pl.pallas_call(
        deliver,
        out_shape=[jax.ShapeDtypeStruct(features.shape, BF)] + [
            jax.ShapeDtypeStruct(s, F32) for s in ((C, 144), (C, C), (C, FF), (C, FF), (2, C))
        ],
        in_specs=[vmem] * 2,
        out_specs=[vmem] * 6,
    )(back, sums)
    return out, d_qkv, d_proj, d_up, d_down.T, d_head.T


def solution(mesh):
    placed = (P("gx", "gy", None), P("gx", "gy", None), P(), P(), P(), P(), P(), P(), P())
    return jax.shard_map(
        body,
        mesh=mesh,
        in_specs=placed,
        out_specs=(P("gx", "gy", None), P(), P(), P(), P(), P()),
        check_vma=False,
    )
```

time: 82.9 us -> 69 us (0.83)
  local copies, waits for them, and re-layouts: 10.7 us -> 0 us
  Pallas kernels: 69.7 us -> 68.2 us
  other arithmetic: 1.32 us -> 0 us
    unnamed x23 -> x0, local copies, waits for them, and re-layouts: 9.14 us -> none
    pallas_call x1 -> x2, Pallas kernels: 69.7 us -> 68.2 us  [the longest x1 66.1 us: body(): pl.pallas_call(make_kernel(nx, ny, tokens), out_shape=[jax.ShapeDtypeStru...]
    reshape x2 -> x0, local copies, waits for them, and re-layouts: 1.39 us -> none  [the longest x1 0.7 us: body(): gain_two.reshape(C, 1)]
where the time goes in v2:
time: 69 us; the launch traced here: 68.8 us
  Pallas kernels  68.2 us (99%)
    pallas_call x1, Pallas kernels, body(): pl.pallas_call(make_kernel(nx, ny, tokens), out_shape=[jax.ShapeDtypeStru...  66.1 us
    pallas_call x1, Pallas kernels, body(): pl.pallas_call(deliver, out_shape=[jax.ShapeDtypeStruct(features.shape, B...  2.07 us

profile of v2, /device:TPU:1, one launch (start us, length us, event | category | flops | bytes accessed | tf_op | source)
XLA Modules:
  0.0 68.8 jit_solution(13927922316294536110)
XLA Ops:
  0.6 66.1 %shard_map.136 = (bf16[7,21,2016]{2,1,0:T(8,128)(2,1)}, f32[48,640]{1,0:T(8,128)}) custom-call(bf16[7,21,2016]{2,1,0:T(8,128)(2,1)} %feat.1, s32[7,21,42]{2,1,0:T(8,128)} %lab.1, bf16[48,144]{1,0:T(8,128)(2,1)} %wqkv.1, bf16[48,48]{1,0:T(8,128)(2,1)} %wproj.1, bf16[48,192]{1,0:T(8,128)(2,1)} %wup.1, bf16[48,192]{1,0:T(8,128)(2,1)} %bitcast.6, ...), custom_call_target="tpu_custom_call" | custom-call | tf_op jit(solution)/shard_map/pallas_call | solution.py:563
  66.8 2.1 %shard_map.137 = (bf16[7,21,2016]{2,1,0:T(8,128)(2,1)}, f32[48,144]{1,0:T(8,128)}, f32[48,48]{1,0:T(8,128)}, f32[48,192]{1,0:T(8,128)}, f32[48,192]{1,0:T(8,128)}, /*index=5*/f32[2,48]{1,0:T(2,128)}) custom-call(bf16[7,21,2016]{2,1,0:T(8,128)(2,1)} %get-tuple-element.14.back, f32[48,640]{1,0:T(8,128)} %get-tuple-element.15.sums), custom_call_target="tpu_custom_call" | custom-call | tf_op jit(solution)/shard_map/pallas_call | solution.py:578

commit v3 on v2

--- a/solution.py
+++ b/solution.py
@@ -52,10 +52,13 @@
       a_up=pltpu.VMEM((C,FF),F32), a_down=pltpu.VMEM((C,FF),F32), a_qkv=pltpu.VMEM((C,144),F32), a_proj=pltpu.VMEM((C,C),F32), a_head=pltpu.VMEM((C,128),F32),
     )
 def win_scratch():
-    return dict(qblk=pltpu.VMEM((240,2304),BF), oblk=pltpu.VMEM((256,2304),BF), P=pltpu.VMEM((KP,2304),BF), D=pltpu.VMEM((KP,2304),BF),
-       qt=pltpu.VMEM((2304,128),BF), ot=pltpu.VMEM((2304,128),BF), dkv=pltpu.VMEM((TL,256),BF))
-
-def init(S, Ws, wqkv, wproj, wup, wdownT, whT, g1, g2):
+    return dict(oblk=pltpu.VMEM((256,2304),BF), P=pltpu.VMEM((KP,2304),BF),
+       qt=pltpu.VMEM((2304,128),BF), ot=pltpu.VMEM((2304,128),BF), tokv=pltpu.VMEM((TL,256),BF), kT=pltpu.VMEM((96,TL),BF), n1=pltpu.VMEM((C,2*TL),BF))
+
+def tmp_scratch():
+    return dict(qblk=pltpu.VMEM((240,2304),BF), D=pltpu.VMEM((KP,2304),BF), dkv=pltpu.VMEM((TL,256),BF))
+
+def init(S, Ws, Ts, wqkv, wproj, wup, wdownT, whT, g1, g2):
     S['qkvT'][...]=wqkv[...].T
     S['projT'][...]=wproj[...].T
     S['upT'][...]=wup[...].T
@@ -87,9 +90,14 @@
     S['g1'][...]=cols[0:C,0:1]; S['g2'][...]=cols[0:C,1:2]; S['wd'][...]=cols[0:C,2:3]
     for k in ('a_up','a_down','a_qkv','a_proj','a_head'): S[k][...]=jnp.zeros(S[k].shape,F32)
     for w in Ws:
-        w['qblk'][...]=jnp.zeros((240,2304),BF)
         w['oblk'][...]=jnp.zeros((256,2304),BF)
-        w['dkv'][...]=jnp.zeros((TL,256),BF)
+    for t in Ts:
+        t['qblk'][...]=jnp.zeros((240,2304),BF)
+        t['dkv'][...]=jnp.zeros((TL,256),BF)
+
+def lane_mask(l0):
+    lane=lax.broadcasted_iota(jnp.int32,(1,128),1)
+    return jnp.where((lane>=l0)&(lane<l0+16),1.0,0.0).astype(BF)
 
 def split2(v):
     a=v.astype(BF); return a,(v-a.astype(F32)).astype(BF)
@@ -104,7 +112,7 @@
 def heads_of(c):
     return slice(16*(256*c//TL),16*((256*c+255)//TL)+16)
 
-def window(out, x, sign, act, S, W, wqkv, wproj, wup):
+def window(out, x, sign, act, S, W, T, wproj, wup):
     x=x()
     g1=S['g1'][...]; g2=S['g2'][...]; wd=S['wd'][...]
     n1=(norm(x)[0]*g1).astype(BF)
@@ -116,25 +124,28 @@
     yield
     qs=split2(packT[0:48].astype(F32)*LOG2E_4)
     r=lax.broadcasted_iota(jnp.int32,(16,1),0)
-    lane=lax.broadcasted_iota(jnp.int32,(1,128),1)
+    W['n1'][...]=n1
+    W['tokv'][...]=tok[:,256:512]
+    for w in range(2):
+        W['kT'][48*w:48*w+48,:]=packT[48:96,TL*w:TL*w+TL]
+    yield
     for w in range(2):
         sc=jnp.where(r<2,act[0],jnp.where(r<4,act[1],jnp.where(r<6,act[2+w],1.0)))
         qm=(S['qmask'][...]*sc).astype(BF)
-        qtok=tok[:,256+128*w:384+128*w].astype(F32)
+        qtok=tok[:,256+128*w:384+128*w]
         for h in range(NH):
             k=3*w+h; ls=slice(k*TL,(k+1)*TL)
             for i in range(2):
-                W['qblk'][128*w+48*i+16*h:128*w+48*i+16*h+16,ls]=qs[i][16*h:16*h+16,TL*w:TL*w+TL]
-            W['qblk'][128*w+96:128*w+112,ls]=qm
+                T['qblk'][128*w+48*i+16*h:128*w+48*i+16*h+16,ls]=qs[i][16*h:16*h+16,TL*w:TL*w+TL]
+            T['qblk'][128*w+96:128*w+112,ls]=qm
             l0=64*(1-w)+16*h
-            W['qt'][ls,:]=jnp.where((lane>=l0)&(lane<l0+16),qtok,0.0).astype(BF)
+            W['qt'][ls,:]=qtok*lane_mask(l0)
             yield
     tk=tok[:KP]
     vT=jnp.concatenate([packT[96:144,0:KP],packT[96:144,TL:TL+KP]],axis=0)
-    kT=jnp.concatenate([packT[48:96,0:KP],packT[48:96,TL:TL+KP]],axis=0)
     def fwd_dot(c):
         rs=slice(0,112) if c<4 else (slice(0,240) if c==4 else slice(128,240))
-        return jnp.exp2(dot(tk[:,rs],W['qblk'][rs,256*c:256*c+256]))
+        return jnp.exp2(dot(tk[:,rs],T['qblk'][rs,256*c:256*c+256]))
     mixp=[]
     p=fwd_dot(0)
     for c in range(9):
@@ -187,7 +198,7 @@
     dO=dot(wproj[...],dst).astype(BF)
     yield
     zr=jnp.zeros((16,TL),BF)
-    dOtok=jnp.concatenate([dO[:,TL:],zr,dO[:,0:TL],zr],axis=0).T.astype(F32)
+    dOtok=jnp.concatenate([dO[:,TL:],zr,dO[:,0:TL],zr],axis=0).T
     yield
     pr=mixf*dO.astype(F32)
     r16=lax.broadcasted_iota(jnp.int32,(16,TL),0)
@@ -198,11 +209,14 @@
             W['oblk'][o+16*h:o+16*h+16,ls]=dO[16*h:16*h+16,ws]
             W['oblk'][o+48:o+64,ls]=jnp.where(r16==0,d0.astype(F32),jnp.where(r16==1,d1.astype(F32),jnp.where(r16==2,d2.astype(F32),0.0))).astype(BF)
             l0=64*(1-w)+16*h
-            W['ot'][ls,:]=jnp.where((lane>=l0)&(lane<l0+16),dOtok,0.0).astype(BF)
+            W['ot'][ls,:]=dOtok*lane_mask(l0)
             yield
+    out(dst)
+
+def backward(out, S, W, T):
     def bwd_dot(c):
         rs=slice(0,64) if c<4 else (slice(0,256) if c==4 else slice(128,256))
-        return dot(tk[:,rs.start+256:rs.stop+256],W['oblk'][rs,256*c:256*c+256]).astype(BF)
+        return dot(W['tokv'][0:KP,rs],W['oblk'][rs,256*c:256*c+256]).astype(BF)
     dqp=[]
     dp=bwd_dot(0)
     for c in range(9):
@@ -210,21 +224,31 @@
         nxt=bwd_dot(c+1) if c<8 else None
         cs=slice(256*c,256*c+256)
         ds=W['P'][:,cs]*dp
-        W['D'][:,cs]=ds
+        T['D'][:,cs]=ds
         yield
-        dqp.append(dot(kT[heads_of(c)],ds))
+        dqp.append(dot(W['kT'][heads_of(c),0:KP],ds))
         dp=nxt
     dq=(0.25*spread(dqp)).astype(BF)
     yield
-    W['dkv'][0:KP,128:256]=dot(W['P'][...],W['ot'][...]).astype(BF)
-    yield
-    W['dkv'][0:KP,0:128]=(0.25*dot(W['D'][...],W['qt'][...])).astype(BF)
-    yield
-    dk=W['dkv'][:,0:128].T; dv=W['dkv'][:,128:256].T
+    def over_queries(a,b):
+        t=None
+        for i in range(3):
+            ks=slice(768*i,768*i+768)
+            d=dot(a[:,ks],b[ks,:])
+            t=d if t is None else t+d
+            yield t
+    for t in over_queries(W['P'],W['ot']):
+        yield
+    T['dkv'][0:KP,128:256]=t.astype(BF)
+    for t in over_queries(T['D'],W['qt']):
+        yield
+    T['dkv'][0:KP,0:128]=(0.25*t).astype(BF)
+    yield
+    dk=T['dkv'][:,0:128].T; dv=T['dkv'][:,128:256].T
     dpack=jnp.concatenate([dq,jnp.concatenate([dk[64:112],dk[0:48]],axis=1),jnp.concatenate([dv[64:112],dv[0:48]],axis=1)],axis=0)
     yield
-    S['a_qkv'][...]+=dot_t(n1,dpack)
-    out(dpack,dst)
+    S['a_qkv'][...]+=dot_t(W['n1'][...],dpack)
+    out(dpack)
 
 def finish(x, dpack, dst, S, wqkv):
     g1=S['g1'][...]
@@ -233,29 +257,32 @@
     return (dst.astype(F32)+norm_back(dn1*g1,xh1,r1)).astype(BF)
 
 
-def drive(gens, stagger=0):
-    live=[]
-    pend=list(gens); k=0
-    while pend or live:
-        if pend and (k>=stagger or not live):
-            live.append(pend.pop(0)); k=0
-            if stagger==0:
-                live+=pend; pend=[]
-        k+=1
-        nxt=[]
-        for g in live:
-            try:
-                next(g); nxt.append(g)
-            except StopIteration: pass
-        live=nxt
+def drive(timed):
+    t=0
+    live=list(timed)
+    while live:
+        left=[]
+        for start,g in live:
+            if t>=start:
+                try:
+                    next(g)
+                except StopIteration:
+                    continue
+            left.append((start,g))
+        live=left
+        t+=1
 
 
 G1 = 8
 G2 = 16
 ROWS = 32
+TWO = sorted(
+    ((a, b) for a in range(4) for b in range(4) if a or b), key=lambda s: -sum(min(v, 4 - v) for v in s)
+)
 NP = 3
 S_KEYS = tuple(scratch())
 W_KEYS = tuple(win_scratch())
+T_KEYS = tuple(tmp_scratch())
 
 
 def comm_scratch(nx, ny):
@@ -314,7 +341,9 @@
         S = dict(zip(S_KEYS, refs))
         refs = refs[len(S_KEYS):]
         Ws = [dict(zip(W_KEYS, refs[i * len(W_KEYS):])) for i in range(NP)]
-        Q = dict(zip(c_keys, refs[NP * len(W_KEYS):]))
+        refs = refs[NP * len(W_KEYS):]
+        Ts = [dict(zip(T_KEYS, refs[i * len(T_KEYS):])) for i in range(NP)]
+        Q = dict(zip(c_keys, refs[NP * len(T_KEYS):]))
         mx = lax.axis_index("gx")
         my = lax.axis_index("gy")
 
@@ -332,9 +361,13 @@
             c2 = lax.rem(core + k % 2, 2)
             return x2 * 2 + c2, ((x2 * 2 + half) * 2 + c2, my)
 
+        z = half * 2 + lax.div(my, 4)
+        y = lax.rem(my, 4)
+
         def in_two(k):
-            h2 = lax.rem(half + k // ny, 2)
-            return ((px * 2 + h2) * 2 + core, lax.rem(my + k % ny, ny))
+            dz, dy = TWO[k - 1]
+            z2, y2 = lax.rem(z + dz, 4), lax.rem(y + dy, 4)
+            return ((px * 2 + lax.div(z2, 2)) * 2 + core, lax.rem(z2, 2) * 4 + y2)
 
         barrier = pltpu.get_barrier_semaphore()
         peers = [at(1, 0), at(-1, 0), at(1, 1), at(-1, -1)]
@@ -343,34 +376,40 @@
             pl.semaphore_signal(barrier, inc=1, device_id=p, device_id_type=MESH)
 
         grid = Q["grid"]
-        grid[:, 0:21, 0:WIDTH] = feat[...].astype(F32)
-        grid[:, 0:21, WIDTH:LAB] = jnp.zeros((WIN, 21, LAB - WIDTH), F32)
-        grid[:, 0:21, LAB:LW] = jnp.zeros((WIN, 21, LW - LAB), F32)
-        grid[:, 0:21, LAB:LAB + DEPTH] = lab[...].astype(F32)
         tmp = Q["rows"]
-        for wy in range(NWY):
+
+        def widen(x0, x1):
+            n = x1 - x0
+            grid[x0:x1, 0:21, 0:WIDTH] = feat[x0:x1].astype(F32)
+            grid[x0:x1, 0:21, WIDTH:LAB] = jnp.zeros((n, 21, LAB - WIDTH), F32)
+            grid[x0:x1, 0:21, LAB:LW] = jnp.zeros((n, 21, LW - LAB), F32)
+            grid[x0:x1, 0:21, LAB:LAB + DEPTH] = lab[x0:x1].astype(F32)
+
+        def pack(wy):
             n = WIN if wy < 2 else 4
             for k in range(SHIFT):
                 tmp[wy, 7 * k:7 * k + n, :] = grid[k, 7 * wy + 3:7 * wy + 3 + n, :]
             Q["xs"][wy] = tmp[wy, 0:32, :].astype(BF)
+
+        hs, hr = Q["hs"], Q["hr"]
+        xcopy = [remote(Q["xs"].at[w], Q["xr"].at[w], hs.at[w], hr.at[w], at(-1, 0)) for w in range(NWY)]
+        ycopy = remote(Q["ys"], Q["yr"], hs.at[3], hr.at[3], at(0, -1))
+        dcopy = remote(Q["ds"], Q["dr"], hs.at[4], hr.at[4], at(-1, -1))
+        widen(0, SHIFT)
+        pack(0)
+        pl.semaphore_wait(barrier, len(peers))
+        xcopy[0].start()
+        widen(SHIFT, WIN)
+        pack(1)
+        pack(2)
         for k in range(4):
             tmp[0, 3 * k:3 * k + 3, :] = grid[3 + k, 0:3, :]
         Q["ys"][...] = tmp[0, 0:16, :].astype(BF)
         for k in range(SHIFT):
             tmp[1, 3 * k:3 * k + 3, :] = grid[k, 0:3, :]
         Q["ds"][...] = tmp[1, 0:16, :].astype(BF)
-        pl.semaphore_wait(barrier, len(peers))
-        hs, hr = Q["hs"], Q["hr"]
-        xcopy = [remote(Q["xs"].at[w], Q["xr"].at[w], hs.at[w], hr.at[w], at(-1, 0)) for w in range(NWY)]
-        ycopy = remote(Q["ys"], Q["yr"], hs.at[3], hr.at[3], at(0, -1))
-        dcopy = remote(Q["ds"], Q["dr"], hs.at[4], hr.at[4], at(-1, -1))
-        xcopy[0].start()
-        ycopy.start()
-        dcopy.start()
-        xcopy[1].start()
-        xcopy[2].start()
-
-        init(S, Ws, wqkv, wproj, wup, wdown, whead, g1, g2)
+
+        init(S, Ws, Ts, wqkv, wproj, wup, wdown, whead, g1, g2)
         rows = Q["rows"]
         for wy in range(NWY):
             n = WIN if wy < 2 else 4
@@ -383,8 +422,33 @@
         last_y = my == ny - 1
         lanes = lax.broadcasted_iota(jnp.int32, (1, TL), 1)
 
+        xcopy[0].wait()
+        xcopy[1].start()
+        xcopy[2].start()
+        ycopy.start()
+        dcopy.start()
+
+        def send_back(w):
+            return remote(Q["bxs"].at[w], Q["bxr"].at[w], Q["bs"].at[w], Q["br"].at[w], at(1, 0))
+
+        def tail(w):
+            for p in range(NP):
+                v = finish(Q["xwin"][NP * w + p].astype(F32), Q["dpk"][NP * w + p], Q["dst"][NP * w + p], S, wqkv)
+                for i in range(2):
+                    for j in range(WIN):
+                        z = (7 * (2 * p + i) + j + SHIFT) % DEPTH
+                        Q["zt"][C * z:C * z + C, 0:49] = v[:, TL * i + 49 * j:TL * i + 49 * j + 49]
+                    yield
+            flat = Q["zt"][...].T.astype(F32)[0:64, 0:WIDTH]
+            Q["back"][w] = flat
+            yield
+            Q["bxs"][w] = jnp.concatenate([flat[28:49], jnp.zeros((11, WIDTH), F32)], axis=0).astype(BF)
+
         def step(wy, _):
-            remote(Q["xs"].at[wy], Q["xr"].at[wy], hs.at[wy], hr.at[wy], at(-1, 0)).wait()
+            @pl.when(wy > 0)
+            def _():
+                remote(Q["xs"].at[wy], Q["xr"].at[wy], hs.at[wy], hr.at[wy], at(-1, 0)).wait()
+
             rows[wy, 28:49, :] = Q["xr"][wy].astype(F32)[0:21]
 
             @pl.when(wy == 2)
@@ -417,19 +481,29 @@
                     [jnp.where(lanes < PT, 1.0 - 2.0 * m, 0.0) for m in marks], axis=1
                 )
 
-            gens = []
+            gens, later = [], []
             act_y = jnp.logical_and(last_y, wy == 2).astype(F32)
             for p in range(NP):
-                def put(dpack, dst, p=p):
+                def put_dst(dst, p=p):
+                    Q["dst"][NP * wy + p] = dst
+
+                def put_dpk(dpack, p=p):
                     Q["dpk"][NP * wy + p] = dpack
-                    Q["dst"][NP * wy + p] = dst
 
                 def get(p=p):
                     return Q["xwin"][NP * wy + p].astype(F32)
 
                 act = (act_x, act_y, F32(0.0), F32(1.0 if p == NP - 1 else 0.0))
-                gens.append(window(put, get, Q["sg"][p:p + 1, :], act, S, Ws[p], wqkv, wproj, wup))
-            drive(gens, 1)
+                gens.append((p, window(put_dst, get, Q["sg"][p:p + 1, :], act, S, Ws[p], Ts[p], wproj, wup)))
+                later.append((p, backward(put_dpk, S, Ws[p], Ts[p])))
+            before = lax.rem(wy + 2, 3)
+            drive(gens + [(6, tail(before))])
+
+            @pl.when(wy > 0)
+            def _():
+                send_back(before).start()
+
+            drive(later)
             return 0
 
         lax.fori_loop(0, NWY, step, 0)
@@ -453,19 +527,8 @@
         for c in first:
             c.start()
 
-        def tail(wy):
-            for p in range(NP):
-                v = finish(Q["xwin"][NP * wy + p].astype(F32), Q["dpk"][NP * wy + p], Q["dst"][NP * wy + p], S, wqkv)
-                for i in range(2):
-                    for j in range(WIN):
-                        z = (7 * (2 * p + i) + j + SHIFT) % DEPTH
-                        Q["zt"][C * z:C * z + C, 0:49] = v[:, TL * i + 49 * j:TL * i + 49 * j + 49]
-            flat = Q["zt"][...].T.astype(F32)[0:64, 0:WIDTH]
-            Q["back"][wy] = flat
-            Q["bxs"][wy] = jnp.concatenate([flat[28:49], jnp.zeros((11, WIDTH), F32)], axis=0).astype(BF)
-            remote(Q["bxs"].at[wy], Q["bxr"].at[wy], Q["bs"].at[wy], Q["br"].at[wy], at(1, 0)).start()
-
-        tail(2)
+        drive([(0, tail(2))])
+        send_back(2).start()
         back, tmp = Q["back"], Q["tmp"]
         for k in range(4):
             tmp[3 * k:3 * k + 3, :] = back[2, 7 * k + 4:7 * k + 7, :]
@@ -490,9 +553,6 @@
         ]
         for c in second:
             c.start()
-
-        tail(0)
-        tail(1)
 
         outf = Q["outf"]
         for x in range(SHIFT, WIN):
@@ -524,7 +584,7 @@
         for k in range(SHIFT):
             outf[k, 0:3, :] = tmp[16 + 3 * k:16 + 3 * k + 3, :]
         for wy in range(NWY):
-            remote(Q["bxs"].at[wy], Q["bxr"].at[wy], Q["bs"].at[wy], Q["br"].at[wy], at(1, 0)).wait()
+            send_back(wy).wait()
             n = WIN if wy < 2 else 4
             tmp[32:64, :] = Q["bxr"][wy].astype(F32)
             for k in range(SHIFT):
@@ -567,6 +627,7 @@
         out_specs=[vmem] * 2,
         scratch_shapes=list(scratch().values())
         + list(win_scratch().values()) * NP
+        + list(tmp_scratch().values()) * NP
         + list(comm_scratch(nx, ny).values()),
         compiler_params=pltpu.CompilerParams(
             collective_id=0, has_side_effects=True, vmem_limit_bytes=60 * 2**20

time: 69 us -> 65.8 us (0.954)
  Pallas kernels: 68.2 us -> 65.1 us
    pallas_call x1, Pallas kernels: 66.1 us -> 63 us  [body(): pl.pallas_call(make_kernel(nx, ny, tokens), out_shape=[jax.ShapeDtypeStru...]
where the time goes in v3:
time: 65.8 us; the launch traced here: 65.7 us
  Pallas kernels  65.1 us (99%)
    pallas_call x1, Pallas kernels, body(): pl.pallas_call(make_kernel(nx, ny, tokens), out_shape=[jax.ShapeDtypeStru...  63 us
    pallas_call x1, Pallas kernels, body(): pl.pallas_call(deliver, out_shape=[jax.ShapeDtypeStruct(features.shape, B...  2.07 us

profile of v3, /device:TPU:1, one launch (start us, length us, event | category | flops | bytes accessed | tf_op | source)
XLA Modules:
  0.0 65.7 jit_solution(2028456759792452100)
XLA Ops:
  0.6 63.0 %shard_map.136 = (bf16[7,21,2016]{2,1,0:T(8,128)(2,1)}, f32[48,640]{1,0:T(8,128)}) custom-call(bf16[7,21,2016]{2,1,0:T(8,128)(2,1)} %feat.1, s32[7,21,42]{2,1,0:T(8,128)} %lab.1, bf16[48,144]{1,0:T(8,128)(2,1)} %wqkv.1, bf16[48,48]{1,0:T(8,128)(2,1)} %wproj.1, bf16[48,192]{1,0:T(8,128)(2,1)} %wup.1, bf16[48,192]{1,0:T(8,128)(2,1)} %bitcast.6, ...), custom_call_target="tpu_custom_call" | custom-call | tf_op jit(solution)/shard_map/pallas_call | solution.py:623
  63.6 2.1 %shard_map.137 = (bf16[7,21,2016]{2,1,0:T(8,128)(2,1)}, f32[48,144]{1,0:T(8,128)}, f32[48,48]{1,0:T(8,128)}, f32[48,192]{1,0:T(8,128)}, f32[48,192]{1,0:T(8,128)}, /*index=5*/f32[2,48]{1,0:T(2,128)}) custom-call(bf16[7,21,2016]{2,1,0:T(8,128)(2,1)} %get-tuple-element.14.back, f32[48,640]{1,0:T(8,128)} %get-tuple-element.15.sums), custom_call_target="tpu_custom_call" | custom-call | tf_op jit(solution)/shard_map/pallas_call | solution.py:639

commit v4 on v3

--- a/solution.py
+++ b/solution.py
@@ -303,6 +303,8 @@
         back=pltpu.VMEM((NWY, 64, WIDTH), F32),
         bxs=pltpu.VMEM((NWY, 32, WIDTH), BF),
         bxr=pltpu.VMEM((NWY, 32, WIDTH), BF),
+        bzs=pltpu.VMEM((16, WIDTH), BF),
+        bzr=pltpu.VMEM((16, WIDTH), BF),
         bys=pltpu.VMEM((16, WIDTH), BF),
         byr=pltpu.VMEM((16, WIDTH), BF),
         bds=pltpu.VMEM((16, WIDTH), BF),
@@ -313,6 +315,8 @@
         r1=pltpu.VMEM((G1 - 1, ROWS, 128), F32),
         r2=pltpu.VMEM((G2, ROWS, 128), BF),
         total=pltpu.VMEM((G1, ROWS, 128), F32),
+        w1=pltpu.VMEM((G1, 64, 128), BF),
+        w2=pltpu.VMEM((G2, 64, 128), BF),
         hs=pltpu.SemaphoreType.DMA((NWY + 2,)),
         hr=pltpu.SemaphoreType.DMA((NWY + 2,)),
         bs=pltpu.SemaphoreType.DMA((NWY + 2,)),
@@ -323,6 +327,10 @@
         q2=pltpu.SemaphoreType.DMA((G2 - 1,)),
         s3=pltpu.SemaphoreType.DMA((G1 - 1,)),
         q3=pltpu.SemaphoreType.DMA((G1 - 1,)),
+        u1=pltpu.SemaphoreType.DMA((G1 - 1,)),
+        v1=pltpu.SemaphoreType.DMA((G1 - 1,)),
+        u2=pltpu.SemaphoreType.DMA((G2 - 1,)),
+        v2=pltpu.SemaphoreType.DMA((G2 - 1,)),
     )
 
 
@@ -444,14 +452,86 @@
             yield
             Q["bxs"][w] = jnp.concatenate([flat[28:49], jnp.zeros((11, WIDTH), F32)], axis=0).astype(BF)
 
+        def windows_of(w):
+            cols = rows[w].astype(BF).T
+            zero = jnp.zeros((C, TL - PT), BF)
+            zrow = jnp.zeros((1, TL - PT), F32)
+            for p in range(NP):
+                zs = [[(7 * wz + j + SHIFT) % DEPTH for j in range(WIN)] for wz in (2 * p, 2 * p + 1)]
+                halves = [jnp.concatenate([cols[C * z:C * z + C, 0:49] for z in u] + [zero], axis=1) for u in zs]
+                Q["xwin"][NP * w + p] = jnp.concatenate(halves, axis=1)
+                marks = [
+                    jnp.concatenate([cols[LAB + z:LAB + z + 1, 0:49].astype(F32) for z in u] + [zrow], axis=1)
+                    for u in zs
+                ]
+                Q["sg"][p:p + 1, :] = jnp.concatenate(
+                    [jnp.where(lanes < PT, 1.0 - 2.0 * m, 0.0) for m in marks], axis=1
+                )
+                yield
+
+        rows[0, 28:49, :] = Q["xr"][0].astype(F32)[0:21]
+        drive([(0, windows_of(0))])
+
+        part = Q["part"]
+
+        def scatter():
+            copies = []
+            for k in range(1, G1):
+                slot, to = in_one(k)
+                copies.append(remote(part.at[slot], Q["r1"].at[k - 1], Q["s1"].at[k - 1], Q["q1"].at[k - 1], to))
+            return copies
+
+        def first_sums():
+            a_head = jnp.sum(S["a_head"][...], axis=1, keepdims=True)
+            acc = jnp.concatenate(
+                [S["a_up"][...], S["a_down"][...], S["a_proj"][...], a_head, jnp.zeros((C, 79), F32)], axis=1
+            )
+            for j in range(16):
+                if j < 12:
+                    v = acc[16 * (j % 3):16 * (j % 3) + 16, 128 * (j // 3):128 * (j // 3) + 128]
+                else:
+                    v = jnp.zeros((16, 128), F32)
+                part[j // 2, 16 * (j % 2):16 * (j % 2) + 16, :] = v
+
         def step(wy, _):
+            gens, later = [], []
+            act_y = jnp.logical_and(last_y, wy == 2).astype(F32)
+            for p in range(NP):
+                def put_dst(dst, p=p):
+                    Q["dst"][NP * wy + p] = dst
+
+                def put_dpk(dpack, p=p):
+                    Q["dpk"][NP * wy + p] = dpack
+
+                def get(p=p):
+                    return Q["xwin"][NP * wy + p].astype(F32)
+
+                act = (act_x, act_y, F32(0.0), F32(1.0 if p == NP - 1 else 0.0))
+                gens.append((p, window(put_dst, get, Q["sg"][p:p + 1, :], act, S, Ws[p], Ts[p], wproj, wup)))
+                later.append((p, backward(put_dpk, S, Ws[p], Ts[p])))
+            before = lax.rem(wy + 2, 3)
+            drive(gens + [(6, tail(before))])
+
             @pl.when(wy > 0)
             def _():
-                remote(Q["xs"].at[wy], Q["xr"].at[wy], hs.at[wy], hr.at[wy], at(-1, 0)).wait()
-
-            rows[wy, 28:49, :] = Q["xr"][wy].astype(F32)[0:21]
+                send_back(before).start()
 
             @pl.when(wy == 2)
+            def _():
+                first_sums()
+                for c in scatter():
+                    c.start()
+
+            following = lax.rem(wy + 1, 3)
+
+            @pl.when(wy < 2)
+            def _():
+                remote(
+                    Q["xs"].at[following], Q["xr"].at[following], hs.at[following], hr.at[following], at(-1, 0)
+                ).wait()
+                rows[following, 28:49, :] = Q["xr"][following].astype(F32)[0:21]
+
+            @pl.when(wy == 1)
             def _():
                 ycopy.wait()
                 dcopy.wait()
@@ -466,82 +546,24 @@
                     rows[2, 28 + 7 * k + 4:28 + 7 * k + 7, 0:WIDTH] = Q["tmp"][16 + 3 * k:16 + 3 * k + 3, :]
                     rows[2, 28 + 7 * k + 4:28 + 7 * k + 7, LAB:LW] = dl[3 * k:3 * k + 3]
 
-            cols = rows[wy].astype(BF).T
-            zero = jnp.zeros((C, TL - PT), BF)
-            zrow = jnp.zeros((1, TL - PT), F32)
-            for p in range(NP):
-                zs = [[(7 * wz + j + SHIFT) % DEPTH for j in range(WIN)] for wz in (2 * p, 2 * p + 1)]
-                halves = [jnp.concatenate([cols[C * z:C * z + C, 0:49] for z in w] + [zero], axis=1) for w in zs]
-                Q["xwin"][NP * wy + p] = jnp.concatenate(halves, axis=1)
-                marks = [
-                    jnp.concatenate([cols[LAB + z:LAB + z + 1, 0:49].astype(F32) for z in w] + [zrow], axis=1)
-                    for w in zs
-                ]
-                Q["sg"][p:p + 1, :] = jnp.concatenate(
-                    [jnp.where(lanes < PT, 1.0 - 2.0 * m, 0.0) for m in marks], axis=1
-                )
-
-            gens, later = [], []
-            act_y = jnp.logical_and(last_y, wy == 2).astype(F32)
-            for p in range(NP):
-                def put_dst(dst, p=p):
-                    Q["dst"][NP * wy + p] = dst
-
-                def put_dpk(dpack, p=p):
-                    Q["dpk"][NP * wy + p] = dpack
-
-                def get(p=p):
-                    return Q["xwin"][NP * wy + p].astype(F32)
-
-                act = (act_x, act_y, F32(0.0), F32(1.0 if p == NP - 1 else 0.0))
-                gens.append((p, window(put_dst, get, Q["sg"][p:p + 1, :], act, S, Ws[p], Ts[p], wproj, wup)))
-                later.append((p, backward(put_dpk, S, Ws[p], Ts[p])))
-            before = lax.rem(wy + 2, 3)
-            drive(gens + [(6, tail(before))])
-
-            @pl.when(wy > 0)
-            def _():
-                send_back(before).start()
-
-            drive(later)
+            drive(later + [(4, windows_of(following))])
             return 0
 
         lax.fori_loop(0, NWY, step, 0)
 
-        a_head = jnp.sum(S["a_head"][...], axis=1, keepdims=True)
-        acc = jnp.concatenate(
-            [S["a_up"][...], S["a_down"][...], S["a_qkv"][...], S["a_proj"][...], a_head, jnp.zeros((C, 63), F32)],
-            axis=1,
+        w1, w2 = Q["w1"], Q["w2"]
+        mine = S["a_qkv"][...].astype(BF)
+        edge = jnp.concatenate(
+            [mine[16 * g:16 * g + 16, 128:144] for g in range(3)] + [jnp.zeros((16, 80), BF)], axis=1
         )
-        part = Q["part"]
-        for j in range(16):
-            if j < 15:
-                v = acc[16 * (j % 3):16 * (j % 3) + 16, 128 * (j // 3):128 * (j // 3) + 128]
-            else:
-                v = jnp.zeros((16, 128), F32)
-            part[j // 2, 16 * (j % 2):16 * (j % 2) + 16, :] = v
-        first = []
-        for k in range(1, G1):
-            slot, to = in_one(k)
-            first.append(remote(part.at[slot], Q["r1"].at[k - 1], Q["s1"].at[k - 1], Q["q1"].at[k - 1], to))
-        for c in first:
+        w1[m1] = jnp.concatenate([mine[:, 0:128], edge], axis=0)
+        fourth = [
+            remote(w1.at[m1], w1.at[m1], Q["u1"].at[k - 1], Q["v1"].at[k - 1], in_one(k)[1]) for k in range(1, G1)
+        ]
+        for c in fourth:
             c.start()
 
-        drive([(0, tail(2))])
-        send_back(2).start()
-        back, tmp = Q["back"], Q["tmp"]
-        for k in range(4):
-            tmp[3 * k:3 * k + 3, :] = back[2, 7 * k + 4:7 * k + 7, :]
-        for k in range(SHIFT):
-            tmp[16 + 3 * k:16 + 3 * k + 3, :] = back[2, 28 + 7 * k + 4:28 + 7 * k + 7, :]
-        Q["bys"][...] = tmp[0:16, :].astype(BF)
-        Q["bds"][...] = tmp[16:32, :].astype(BF)
-        bycopy = remote(Q["bys"], Q["byr"], Q["bs"].at[3], Q["br"].at[3], at(0, 1))
-        bdcopy = remote(Q["bds"], Q["bdr"], Q["bs"].at[4], Q["br"].at[4], at(1, 1))
-        bycopy.start()
-        bdcopy.start()
-
-        for c in first:
+        for c in scatter():
             c.wait()
         csum = part[m1]
         for k in range(G1 - 1):
@@ -552,6 +574,36 @@
             remote(r2.at[m2], r2.at[m2], Q["s2"].at[k - 1], Q["q2"].at[k - 1], in_two(k)) for k in range(1, G2)
         ]
         for c in second:
+            c.start()
+
+        drive([(0, tail(2))])
+        back, tmp = Q["back"], Q["tmp"]
+        for k in range(4):
+            tmp[3 * k:3 * k + 3, :] = back[2, 7 * k + 4:7 * k + 7, :]
+        for k in range(SHIFT):
+            tmp[16 + 3 * k:16 + 3 * k + 3, :] = back[2, 28 + 7 * k + 4:28 + 7 * k + 7, :]
+        for k in range(SHIFT):
+            tmp[32 + 4 * k:36 + 4 * k, :] = back[2, 28 + 7 * k:28 + 7 * k + 4, :]
+        Q["bzs"][...] = tmp[32:48, :].astype(BF)
+        bzcopy = remote(Q["bzs"], Q["bzr"], Q["bs"].at[2], Q["br"].at[2], at(1, 0))
+        Q["bys"][...] = tmp[0:16, :].astype(BF)
+        Q["bds"][...] = tmp[16:32, :].astype(BF)
+        bycopy = remote(Q["bys"], Q["byr"], Q["bs"].at[3], Q["br"].at[3], at(0, 1))
+        bdcopy = remote(Q["bds"], Q["bdr"], Q["bs"].at[4], Q["br"].at[4], at(1, 1))
+        bzcopy.start()
+        bycopy.start()
+        bdcopy.start()
+
+        for c in fourth:
+            c.wait()
+        s8 = w1[0].astype(F32)
+        for k in range(1, G1):
+            s8 = s8 + w1[k].astype(F32)
+        w2[m2] = s8.astype(BF)
+        fifth = [
+            remote(w2.at[m2], w2.at[m2], Q["u2"].at[k - 1], Q["v2"].at[k - 1], in_two(k)) for k in range(1, G2)
+        ]
+        for c in fifth:
             c.start()
 
         outf = Q["outf"]
@@ -583,25 +635,32 @@
             outf[SHIFT + k, 0:3, :] = tmp[3 * k:3 * k + 3, :]
         for k in range(SHIFT):
             outf[k, 0:3, :] = tmp[16 + 3 * k:16 + 3 * k + 3, :]
-        for wy in range(NWY):
+        for wy in range(2):
             send_back(wy).wait()
-            n = WIN if wy < 2 else 4
             tmp[32:64, :] = Q["bxr"][wy].astype(F32)
             for k in range(SHIFT):
-                outf[k, 7 * wy + 3:7 * wy + 3 + n, :] = tmp[32 + 7 * k:32 + 7 * k + n, :]
+                outf[k, 7 * wy + 3:7 * wy + 10, :] = tmp[32 + 7 * k:39 + 7 * k, :]
+        bzcopy.wait()
+        tmp[32:48, :] = Q["bzr"][...].astype(F32)
+        for k in range(SHIFT):
+            outf[k, 17:21, :] = tmp[32 + 4 * k:36 + 4 * k, :]
         out[...] = outf[:, 0:21, :].astype(BF)
+
+        for c in fifth:
+            c.wait()
+        s16 = w2[0].astype(F32)
+        for k in range(1, G2):
+            s16 = s16 + w2[k].astype(F32)
+        s16 = s16 * (1.0 / math.sqrt(tokens))
+        right = jnp.concatenate([s16[48:64, 16 * g:16 * g + 16] for g in range(3)], axis=0)
+        o_sum[:, 512:768] = jnp.concatenate([s16[0:48], right, jnp.zeros((C, 112), F32)], axis=1)
 
         for c in third:
             c.wait()
-        parts = []
-        for l in range(5):
-            parts.append(
-                jnp.concatenate(
-                    [total[j // 2, 16 * (j % 2):16 * (j % 2) + 16, :] for j in range(3 * l, 3 * l + 3)], axis=0
-                )
+        for l in range(4):
+            o_sum[:, 128 * l:128 * l + 128] = jnp.concatenate(
+                [total[j // 2, 16 * (j % 2):16 * (j % 2) + 16, :] for j in range(3 * l, 3 * l + 3)], axis=0
             )
-        whole = jnp.concatenate(parts, axis=1)
-        o_sum[...] = whole
 
     return kernel
 
@@ -610,9 +669,9 @@
     out[...] = back[...]
     o_up[...] = sums[:, 0:192]
     o_down[...] = sums[:, 192:384]
-    o_qkv[...] = sums[:, 384:528]
-    o_proj[...] = sums[:, 528:576]
-    col = sums[:, 512:640].T[64:65]
+    o_proj[...] = sums[:, 384:432]
+    o_qkv[...] = sums[:, 512:656]
+    col = sums[:, 384:512].T[48:49]
     o_head[...] = jnp.concatenate([-col, col], axis=0)
 
 
@@ -622,7 +681,7 @@
     vmem = pl.BlockSpec(memory_space=pltpu.VMEM)
     back, sums = pl.pallas_call(
         make_kernel(nx, ny, tokens),
-        out_shape=[jax.ShapeDtypeStruct(features.shape, BF), jax.ShapeDtypeStruct((C, 640), F32)],
+        out_shape=[jax.ShapeDtypeStruct(features.shape, BF), jax.ShapeDtypeStruct((C, 768), F32)],
         in_specs=[vmem] * 9,
         out_specs=[vmem] * 2,
         scratch_shapes=list(scratch().values())

time: 65.8 us -> 63.6 us (0.967)
  Pallas kernels: 65.1 us -> 62.8 us
    pallas_call x1, Pallas kernels: 63 us -> 60.7 us  [body(): pl.pallas_call(make_kernel(nx, ny, tokens), out_shape=[jax.ShapeDtypeStru...]
where the time goes in v4:
time: 63.6 us; the launch traced here: 63.5 us
  Pallas kernels  62.8 us (99%)
  between operations  0.64 us (1%)
    pallas_call x1, Pallas kernels, body(): pl.pallas_call(make_kernel(nx, ny, tokens), out_shape=[jax.ShapeDtypeStru...  60.7 us
    pallas_call x1, Pallas kernels, body(): pl.pallas_call(deliver, out_shape=[jax.ShapeDtypeStruct(features.shape, B...  2.08 us

profile of v4, /device:TPU:1, one launch (start us, length us, event | category | flops | bytes accessed | tf_op | source)
XLA Modules:
  0.0 63.5 jit_solution(18379156113784210239)
XLA Ops:
  0.6 60.7 %shard_map.136 = (bf16[7,21,2016]{2,1,0:T(8,128)(2,1)}, f32[48,768]{1,0:T(8,128)}) custom-call(bf16[7,21,2016]{2,1,0:T(8,128)(2,1)} %feat.1, s32[7,21,42]{2,1,0:T(8,128)} %lab.1, bf16[48,144]{1,0:T(8,128)(2,1)} %wqkv.1, bf16[48,48]{1,0:T(8,128)(2,1)} %wproj.1, bf16[48,192]{1,0:T(8,128)(2,1)} %wup.1, bf16[48,192]{1,0:T(8,128)(2,1)} %bitcast.6, ...), custom_call_target="tpu_custom_call" | custom-call | tf_op jit(solution)/shard_map/pallas_call | solution.py:682
  61.4 2.1 %shard_map.137 = (bf16[7,21,2016]{2,1,0:T(8,128)(2,1)}, f32[48,144]{1,0:T(8,128)}, f32[48,48]{1,0:T(8,128)}, f32[48,192]{1,0:T(8,128)}, f32[48,192]{1,0:T(8,128)}, /*index=5*/f32[2,48]{1,0:T(2,128)}) custom-call(bf16[7,21,2016]{2,1,0:T(8,128)(2,1)} %get-tuple-element.14.back, f32[48,768]{1,0:T(8,128)} %get-tuple-element.15.sums), custom_call_target="tpu_custom_call" | custom-call | tf_op jit(solution)/shard_map/pallas_call | solution.py:698

commit v5 on v4

--- a/solution.py
+++ b/solution.py
@@ -280,6 +280,7 @@
     ((a, b) for a in range(4) for b in range(4) if a or b), key=lambda s: -sum(min(v, 4 - v) for v in s)
 )
 NP = 3
+IN_KEYS = ("i_feat", "i_lab", "i_qkv", "i_proj", "i_up", "i_down", "i_head", "i_g1", "i_g2")
 S_KEYS = tuple(scratch())
 W_KEYS = tuple(win_scratch())
 T_KEYS = tuple(tmp_scratch())
@@ -287,6 +288,16 @@
 
 def comm_scratch(nx, ny):
     return dict(
+        i_feat=pltpu.VMEM((WIN, 21, WIDTH), BF),
+        i_lab=pltpu.VMEM((WIN, 21, DEPTH), jnp.int32),
+        i_qkv=pltpu.VMEM((C, 144), BF),
+        i_proj=pltpu.VMEM((C, C), BF),
+        i_up=pltpu.VMEM((C, FF), BF),
+        i_down=pltpu.VMEM((C, FF), BF),
+        i_head=pltpu.VMEM((2, C), BF),
+        i_g1=pltpu.VMEM((1, C), F32),
+        i_g2=pltpu.VMEM((1, C), F32),
+        ins=pltpu.SemaphoreType.DMA((10,)),
         grid=pltpu.VMEM((WIN, 24, LW), F32),
         rows=pltpu.VMEM((NWY, 64, LW), F32),
         xs=pltpu.VMEM((NWY, 32, LW), BF),
@@ -343,7 +354,9 @@
 def make_kernel(nx, ny, tokens):
     c_keys = tuple(comm_scratch(nx, ny))
 
-    def kernel(feat, lab, wqkv, wproj, wup, wdown, whead, g1, g2, *refs):
+    def kernel(*refs):
+        hbm = refs[:9]
+        refs = refs[9:]
         out, o_sum = refs[:2]
         refs = refs[2:]
         S = dict(zip(S_KEYS, refs))
@@ -352,6 +365,8 @@
         refs = refs[NP * len(W_KEYS):]
         Ts = [dict(zip(T_KEYS, refs[i * len(T_KEYS):])) for i in range(NP)]
         Q = dict(zip(c_keys, refs[NP * len(T_KEYS):]))
+        held = [Q[k] for k in IN_KEYS]
+        feat, lab, wqkv, wproj, wup, wdown, whead, g1, g2 = held
         mx = lax.axis_index("gx")
         my = lax.axis_index("gy")
 
@@ -382,6 +397,16 @@
         peers += [in_one(k)[1] for k in range(1, G1)] + [in_two(k) for k in range(1, G2)]
         for p in peers:
             pl.semaphore_signal(barrier, inc=1, device_id=p, device_id_type=MESH)
+
+        ins = Q["ins"]
+        early = [
+            pltpu.make_async_copy(hbm[0].at[0:SHIFT], feat.at[0:SHIFT], ins.at[0]),
+            pltpu.make_async_copy(hbm[1], lab, ins.at[1]),
+        ]
+        late = [pltpu.make_async_copy(hbm[0].at[SHIFT:WIN], feat.at[SHIFT:WIN], ins.at[2])]
+        late += [pltpu.make_async_copy(hbm[i], held[i], ins.at[i + 1]) for i in range(2, 9)]
+        for c in early + late:
+            c.start()
 
         grid = Q["grid"]
         tmp = Q["rows"]
@@ -403,10 +428,14 @@
         xcopy = [remote(Q["xs"].at[w], Q["xr"].at[w], hs.at[w], hr.at[w], at(-1, 0)) for w in range(NWY)]
         ycopy = remote(Q["ys"], Q["yr"], hs.at[3], hr.at[3], at(0, -1))
         dcopy = remote(Q["ds"], Q["dr"], hs.at[4], hr.at[4], at(-1, -1))
+        for c in early:
+            c.wait()
         widen(0, SHIFT)
         pack(0)
         pl.semaphore_wait(barrier, len(peers))
         xcopy[0].start()
+        for c in late:
+            c.wait()
         widen(SHIFT, WIN)
         pack(1)
         pack(2)
@@ -682,7 +711,7 @@
     back, sums = pl.pallas_call(
         make_kernel(nx, ny, tokens),
         out_shape=[jax.ShapeDtypeStruct(features.shape, BF), jax.ShapeDtypeStruct((C, 768), F32)],
-        in_specs=[vmem] * 9,
+        in_specs=[pl.BlockSpec(memory_space=pl.ANY)] * 9,
         out_specs=[vmem] * 2,
         scratch_shapes=list(scratch().values())
         + list(win_scratch().values()) * NP

time: 63.6 us -> 62.7 us (0.986)
  Pallas kernels: 62.8 us -> 61.9 us
    pallas_call x1, Pallas kernels: 60.7 us -> 59.8 us  [body(): pl.pallas_call(make_kernel(nx, ny, tokens), out_shape=[jax.ShapeDtypeStru...]
where the time goes in v5:
time: 62.7 us; the launch traced here: 62.6 us
  Pallas kernels  61.9 us (99%)
  between operations  0.64 us (1%)
    pallas_call x1, Pallas kernels, body(): pl.pallas_call(make_kernel(nx, ny, tokens), out_shape=[jax.ShapeDtypeStru...  59.8 us
    pallas_call x1, Pallas kernels, body(): pl.pallas_call(deliver, out_shape=[jax.ShapeDtypeStruct(features.shape, B...  2.08 us

profile of v5, /device:TPU:1, one launch (start us, length us, event | category | flops | bytes accessed | tf_op | source)
XLA Modules:
  0.0 62.6 jit_solution(7370428337710885262)
XLA Ops:
  0.6 59.8 %shard_map.136 = (bf16[7,21,2016]{2,1,0:T(8,128)(2,1)}, f32[48,768]{1,0:T(8,128)}) custom-call(bf16[7,21,2016]{2,1,0:T(8,128)(2,1)} %refs_0_.1, s32[7,21,42]{2,1,0:T(8,128)} %refs_1_.1, bf16[48,144]{1,0:T(8,128)(2,1)} %refs_2_.1, bf16[48,48]{1,0:T(8,128)(2,1)} %refs_3_.1, bf16[48,192]{1,0:T(8,128)(2,1)} %refs_4_.1, bf16[48,192]{1,0:T(8,128)(2,1)} %bitcast.6, ...), custom_call_target="tpu_custom_call" | custom-call | tf_op jit(solution)/shard_map/pallas_call | solution.py:711
  60.5 2.1 %shard_map.137 = (bf16[7,21,2016]{2,1,0:T(8,128)(2,1)}, f32[48,144]{1,0:T(8,128)}, f32[48,48]{1,0:T(8,128)}, f32[48,192]{1,0:T(8,128)}, f32[48,192]{1,0:T(8,128)}, /*index=5*/f32[2,48]{1,0:T(2,128)}) custom-call(bf16[7,21,2016]{2,1,0:T(8,128)(2,1)} %get-tuple-element.14.back, f32[48,768]{1,0:T(8,128)} %get-tuple-element.15.sums), custom_call_target="tpu_custom_call" | custom-call | tf_op jit(solution)/shard_map/pallas_call | solution.py:727
